TPU v7x, 32 devices: a whole 2x2x4 slice. The times are simulated.
32 devices in a mesh: clip: 8 (over y, x, core), frame: 4 (over z).
Axes of the slice: x: 2, y: 2, z: 4, core: 2. Of those that a mesh axis runs over, the one named last changes fastest.
Arguments:
- tokens: bfloat16 [32, 4, 256, 768], P('clip', 'frame'), may hold values from -6 to 6
- target: bfloat16 [32, 4, 256, 768], P('clip', 'frame'), may hold values from -6 to 6
- loss_weight: float32 [32], P('clip'), may hold values from 0.5 to 2
- timesteps: int32 [32], replicated, may hold values from 0 to 999
- offsets: int32 [32], P('clip'), may hold values from 0 to 63
- cond_table: float32 [1000, 768], replicated, may hold values from -6 to 6
- modulate_w: bfloat16 [768, 6912], replicated, may hold values from -0.21875 to 0.21875
- spatial_qkv: bfloat16 [768, 2304], replicated, may hold values from -0.21875 to 0.21875
- spatial_out: bfloat16 [768, 768], replicated, may hold values from -0.875 to 0.875
- temporal_qkv: bfloat16 [768, 2304], replicated, may hold values from -0.21875 to 0.21875
- temporal_out: bfloat16 [768, 768], replicated, may hold values from -0.3125 to 0.3125
- mlp_in: bfloat16 [768, 3072], replicated, may hold values from -0.21875 to 0.21875
- mlp_out: bfloat16 [3072, 768], replicated, may hold values from -0.109375 to 0.109375
Outputs:
- output: bfloat16 [32, 4, 256, 768], P('clip', 'frame')
- grad_tokens: float32 [32, 4, 256, 768], P('clip', 'frame')
- grad_table: float32 [1000, 768], replicated
- grad_modulate: float32 [768, 6912], P('clip', 'frame')
- grad_spatial_qkv: float32 [768, 2304], P('clip', 'frame')
- grad_spatial_out: float32 [768, 768], P('clip', 'frame')
- grad_temporal_qkv: float32 [768, 2304], P('clip', 'frame')
- grad_temporal_out: float32 [768, 768], P('clip', 'frame')
- grad_mlp_in: float32 [768, 3072], P('clip', 'frame')
- grad_mlp_out: float32 [3072, 768], P('clip', 'frame')
All inputs are finite; a program needn't handle non-finite values.
Results may differ from a plain program's by a relative error of at most 0.012.
The roundings to bfloat16 on the way count: a program that leaves them out, or rounds other values in their place, can miss the bound.
Values may be sent and summed in bfloat16 or wider, within the bound.
A program may use at most 256 MiB of HBM per device.

v0:
```python
from functools import partial
import math

import jax
import jax.numpy as jnp
from jax import lax
from jax.sharding import PartitionSpec as P

HEAD_DIM = 64
STEPS = 1000


NORM_EPSILON = 1e-06
HIGHEST_PRECISION = lax.Precision.HIGHEST


def padded(shard, sides, width):
    for axis, dim in sides:
        count, length = (lax.axis_size(axis), shard.shape[dim])
        up = [(i, (i + 1) % count) for i in range(count - 1)]
        down = [(j, i) for i, j in up]
        last = lax.slice_in_dim(shard, length - width, length, axis=dim)
        first = lax.slice_in_dim(shard, 0, width, axis=dim)
        before = lax.ppermute(last, axis, up)
        after = lax.ppermute(first, axis, down)
        shard = jnp.concatenate([before, shard, after], axis=dim)
    return shard


def layer_norm(values):
    centred = values - jnp.mean(values, axis=-1, keepdims=True)
    inv_std = lax.rsqrt(jnp.mean(centred * centred, axis=-1, keepdims=True) + NORM_EPSILON)
    return (centred * inv_std, inv_std)


def norm_back(grad_hidden, normed, inv_std, scale_mod):
    grad_normed = grad_hidden * (1.0 + scale_mod)
    mean_grad = jnp.mean(grad_normed, axis=-1, keepdims=True)
    mean_cross = jnp.mean(grad_normed * normed, axis=-1, keepdims=True)
    return inv_std * (grad_normed - mean_grad - normed * mean_cross)


def token_sum(values):
    return jnp.sum(values, axis=(1, 2))


def contract_rows(left, right):
    return lax.dot_general(
        left, right, (((0,), (0,)), ((), ())), preferred_element_type=jnp.float32
    )


def contract_cols(left, right):
    return lax.dot_general(
        left, right, (((1,), (1,)), ((), ())), preferred_element_type=jnp.float32
    )


def split_dot(left, right_low):
    high_part = left.astype(jnp.bfloat16)
    remainder = left - high_part.astype(jnp.float32)
    mid_part = remainder.astype(jnp.bfloat16)
    low_part = (remainder - mid_part.astype(jnp.float32)).astype(jnp.bfloat16)
    summed = contract_cols(high_part, right_low) + contract_cols(mid_part, right_low)
    return summed + contract_cols(low_part, right_low)


def local(
    tokens,
    target,
    loss_weight,
    timesteps,
    offsets,
    cond_table,
    modulate_w,
    spatial_qkv,
    spatial_out,
    temporal_qkv,
    temporal_out,
    mlp_in,
    mlp_out,
):
    clips_here, frames_here, patches, model_width = tokens.shape
    head_count = model_width // HEAD_DIM
    rows_here = clips_here * frames_here * patches
    scale_qk = HEAD_DIM ** (-0.5)
    frame_start = lax.axis_index("frame") * frames_here
    all_frames = frames_here * lax.axis_size("frame")
    clip_start = lax.axis_index("clip") * clips_here
    step_ids = jnp.arange(STEPS, dtype=jnp.int32)
    local_steps = lax.dynamic_slice_in_dim(timesteps, clip_start, clips_here)
    onehot_local = (local_steps[:, None] == step_ids[None, :]).astype(jnp.float32)
    condition = jnp.dot(onehot_local, cond_table, precision=HIGHEST_PRECISION)
    cond_act, silu_pull = jax.vjp(jax.nn.silu, condition)
    cond_low = cond_act.astype(jnp.bfloat16)
    modulation = jnp.dot(cond_low, modulate_w, preferred_element_type=jnp.float32)
    modulation = modulation.reshape(clips_here, 9, 1, 1, model_width)
    mod_parts = [modulation[:, number] for number in range(9)]
    inputs = tokens.astype(jnp.float32)
    normed_a, inv_a = layer_norm(inputs)
    hidden_a = (
        (normed_a * (1.0 + mod_parts[1]) + mod_parts[0])
        .astype(jnp.bfloat16)
        .reshape(rows_here, model_width)
    )
    proj_a = jnp.dot(hidden_a, spatial_qkv, preferred_element_type=jnp.float32).astype(jnp.bfloat16)
    proj_a = proj_a.reshape(clips_here * frames_here, patches, 3, head_count, HEAD_DIM)
    queries_a, keys_a, values_a = (proj_a[:, :, 0], proj_a[:, :, 1], proj_a[:, :, 2])

    def spatial_scores():
        return (
            jnp.einsum("nqhd,nkhd->nhqk", queries_a, keys_a, preferred_element_type=jnp.float32)
            * scale_qk
        )

    scores_a = spatial_scores()
    log_total = jax.nn.logsumexp(scores_a, axis=-1, keepdims=True)
    soft_low_a = jnp.exp(scores_a - log_total).astype(jnp.bfloat16)
    mixed_a = jnp.einsum(
        "nhqk,nkhd->nqhd", soft_low_a, values_a, preferred_element_type=jnp.float32
    )
    mixed_a = mixed_a.astype(jnp.bfloat16).reshape(rows_here, model_width)
    branch_a = jnp.dot(mixed_a, spatial_out, preferred_element_type=jnp.float32).reshape(
        tokens.shape
    )
    after_a = inputs + mod_parts[2] * branch_a
    normed_b, inv_b = layer_norm(after_a)
    half_width = model_width // 2
    positions = (
        offsets[:, None] + frame_start + jnp.arange(frames_here, dtype=jnp.int32)[None, :]
    ).astype(jnp.float32)
    freqs = jnp.exp(jnp.arange(half_width, dtype=jnp.float32) * (-math.log(10000.0) / half_width))
    angles = positions[:, :, None] * freqs
    posenc = jnp.concatenate((jnp.sin(angles), jnp.cos(angles)), axis=-1)[:, :, None, :]
    hidden_b = (
        (normed_b * (1.0 + mod_parts[4]) + mod_parts[3] + posenc)
        .astype(jnp.bfloat16)
        .reshape(rows_here, model_width)
    )
    proj_b = jnp.dot(hidden_b, temporal_qkv, preferred_element_type=jnp.float32).astype(
        jnp.bfloat16
    )
    proj_b = proj_b.reshape(clips_here, frames_here, patches, 3 * model_width)
    queries_b = proj_b[..., :model_width]
    stacked = jnp.stack(
        (proj_b[..., model_width : 2 * model_width], proj_b[..., 2 * model_width :])
    )
    extended = padded(stacked, (("frame", 2),), 1)
    head_shape = (clips_here, frames_here, patches, head_count, HEAD_DIM)
    queries_f = queries_b.astype(jnp.float32).reshape(head_shape)
    key_list = []
    value_list = []
    score_list = []
    for offset_key in range(3):
        key_here = (
            extended[0, :, offset_key : offset_key + frames_here]
            .astype(jnp.float32)
            .reshape(head_shape)
        )
        value_here = (
            extended[1, :, offset_key : offset_key + frames_here]
            .astype(jnp.float32)
            .reshape(head_shape)
        )
        key_frame = frame_start + jnp.arange(frames_here, dtype=jnp.int32) + offset_key - 1
        key_ok = (key_frame >= 0) & (key_frame < all_frames)
        raw = jnp.sum(queries_f * key_here, axis=-1) * scale_qk
        score_list.append(jnp.where(key_ok[None, :, None, None], raw, -1e30))
        key_list.append(key_here)
        value_list.append(value_here)
    soft_b = jax.nn.softmax(jnp.stack(score_list), axis=0)
    soft_low_b = soft_b.astype(jnp.bfloat16).astype(jnp.float32)
    mixed_sum = soft_low_b[0][..., None] * value_list[0]
    for offset_key in range(1, 3):
        mixed_sum = mixed_sum + soft_low_b[offset_key][..., None] * value_list[offset_key]
    mixed_b = mixed_sum.reshape(rows_here, model_width).astype(jnp.bfloat16)
    branch_b = jnp.dot(mixed_b, temporal_out, preferred_element_type=jnp.float32).reshape(
        tokens.shape
    )
    after_b = after_a + mod_parts[5] * branch_b
    normed_c, inv_c = layer_norm(after_b)
    hidden_c = (
        (normed_c * (1.0 + mod_parts[7]) + mod_parts[6])
        .astype(jnp.bfloat16)
        .reshape(rows_here, model_width)
    )
    upward = jnp.dot(hidden_c, mlp_in, preferred_element_type=jnp.float32)
    act_value, gelu_pull = jax.vjp(partial(jax.nn.gelu, approximate=True), upward)
    act_low = act_value.astype(jnp.bfloat16)
    branch_c = jnp.dot(act_low, mlp_out, preferred_element_type=jnp.float32).reshape(tokens.shape)
    result = after_b + mod_parts[8] * branch_c
    output = result.astype(jnp.bfloat16)
    grad_result = loss_weight[:, None, None, None] * (result - target.astype(jnp.float32))
    grad_gate_c = token_sum(grad_result * branch_c)
    grad_branch_c = (
        (mod_parts[8] * grad_result).astype(jnp.bfloat16).reshape(rows_here, model_width)
    )
    grad_act = contract_cols(grad_branch_c, mlp_out)
    weight_mlp_out = contract_rows(act_low, grad_branch_c)
    grad_upward = gelu_pull(grad_act)[0].astype(jnp.bfloat16)
    weight_mlp_in = contract_rows(hidden_c, grad_upward)
    grad_hidden_c = contract_cols(grad_upward, mlp_in).reshape(tokens.shape)
    grad_shift_c = token_sum(grad_hidden_c)
    grad_scale_c = token_sum(grad_hidden_c * normed_c)
    grad_after_b = grad_result + norm_back(grad_hidden_c, normed_c, inv_c, mod_parts[7])
    grad_gate_b = token_sum(grad_after_b * branch_b)
    grad_branch_b = (
        (mod_parts[5] * grad_after_b).astype(jnp.bfloat16).reshape(rows_here, model_width)
    )
    grad_mixed_b = contract_cols(grad_branch_b, temporal_out).astype(jnp.bfloat16)
    weight_temporal_out = contract_rows(mixed_b, grad_branch_b)
    grad_mixed_f = grad_mixed_b.astype(jnp.float32).reshape(head_shape)
    grad_soft = jnp.stack(
        [jnp.sum(grad_mixed_f * value_list[offset_key], axis=-1) for offset_key in range(3)]
    )
    inner_soft = jnp.sum(soft_b * grad_soft, axis=0)
    grad_scores_b = (soft_b * (grad_soft - inner_soft)).astype(jnp.bfloat16).astype(
        jnp.float32
    ) * scale_qk
    grad_queries_b = grad_scores_b[0][..., None] * key_list[0]
    grad_keys_ext = jnp.zeros((clips_here, frames_here + 2, patches, model_width), jnp.float32)
    grad_values_ext = jnp.zeros((clips_here, frames_here + 2, patches, model_width), jnp.float32)
    flat_shape = (clips_here, frames_here, patches, model_width)
    for offset_key in range(3):
        if offset_key > 0:
            grad_queries_b = (
                grad_queries_b + grad_scores_b[offset_key][..., None] * key_list[offset_key]
            )
        pad_spec = ((0, 0), (offset_key, 2 - offset_key), (0, 0), (0, 0))
        key_term = (grad_scores_b[offset_key][..., None] * queries_f).reshape(flat_shape)
        value_term = (soft_low_b[offset_key][..., None] * grad_mixed_f).reshape(flat_shape)
        grad_keys_ext = grad_keys_ext + jnp.pad(key_term, pad_spec)
        grad_values_ext = grad_values_ext + jnp.pad(value_term, pad_spec)
    stacked_grads = jnp.stack((grad_keys_ext, grad_values_ext))
    rim_grads = jnp.concatenate(
        (stacked_grads[:, :, :1], stacked_grads[:, :, frames_here + 1 :]), axis=2
    )
    returned = padded(rim_grads.astype(jnp.bfloat16), (("frame", 2),), 1).astype(rim_grads.dtype)
    owned = stacked_grads[:, :, 1 : frames_here + 1]
    owned = owned.at[:, :, 0].add(returned[:, :, 0])
    owned = owned.at[:, :, frames_here - 1].add(returned[:, :, 3])
    grad_proj_b = jnp.concatenate((grad_queries_b.reshape(flat_shape), owned[0], owned[1]), axis=-1)
    grad_proj_b = grad_proj_b.astype(jnp.bfloat16).reshape(rows_here, 3 * model_width)
    weight_temporal_qkv = contract_rows(hidden_b, grad_proj_b)
    grad_hidden_b = contract_cols(grad_proj_b, temporal_qkv).reshape(tokens.shape)
    grad_shift_b = token_sum(grad_hidden_b)
    grad_scale_b = token_sum(grad_hidden_b * normed_b)
    grad_after_a = grad_after_b + norm_back(grad_hidden_b, normed_b, inv_b, mod_parts[4])
    grad_gate_a = token_sum(grad_after_a * branch_a)
    grad_branch_a = (
        (mod_parts[2] * grad_after_a).astype(jnp.bfloat16).reshape(rows_here, model_width)
    )
    grad_mixed_a = contract_cols(grad_branch_a, spatial_out).astype(jnp.bfloat16)
    weight_spatial_out = contract_rows(mixed_a, grad_branch_a)
    grad_mixed_a = grad_mixed_a.reshape(clips_here * frames_here, patches, head_count, HEAD_DIM)
    soft_again = jnp.exp(spatial_scores() - log_total)
    soft_again_low = soft_again.astype(jnp.bfloat16)
    grad_soft_a = jnp.einsum(
        "nqhd,nkhd->nhqk", grad_mixed_a, values_a, preferred_element_type=jnp.float32
    )
    inner_a = jnp.sum(soft_again * grad_soft_a, axis=-1, keepdims=True)
    grad_scores_a = (soft_again * (grad_soft_a - inner_a)).astype(jnp.bfloat16)
    grad_queries_a = (
        jnp.einsum("nhqk,nkhd->nqhd", grad_scores_a, keys_a, preferred_element_type=jnp.float32)
        * scale_qk
    )
    grad_keys_a = (
        jnp.einsum("nhqk,nqhd->nkhd", grad_scores_a, queries_a, preferred_element_type=jnp.float32)
        * scale_qk
    )
    grad_values_a = jnp.einsum(
        "nhqk,nqhd->nkhd", soft_again_low, grad_mixed_a, preferred_element_type=jnp.float32
    )
    grad_proj_a = jnp.stack((grad_queries_a, grad_keys_a, grad_values_a), axis=2)
    grad_proj_a = grad_proj_a.astype(jnp.bfloat16).reshape(rows_here, 3 * model_width)
    weight_spatial_qkv = contract_rows(hidden_a, grad_proj_a)
    grad_hidden_a = contract_cols(grad_proj_a, spatial_qkv).reshape(tokens.shape)
    grad_shift_a = token_sum(grad_hidden_a)
    grad_scale_a = token_sum(grad_hidden_a * normed_a)
    grad_inputs = grad_after_a + norm_back(grad_hidden_a, normed_a, inv_a, mod_parts[1])
    grad_modulation = jnp.stack(
        (
            grad_shift_a,
            grad_scale_a,
            grad_gate_a,
            grad_shift_b,
            grad_scale_b,
            grad_gate_b,
            grad_shift_c,
            grad_scale_c,
            grad_gate_c,
        ),
        axis=1,
    )
    grad_modulation = grad_modulation.reshape(clips_here, 9 * model_width)
    cond_wide = cond_low.astype(jnp.float32)
    grad_condition = silu_pull(split_dot(grad_modulation, modulate_w))[0]
    local_table = lax.dot_general(
        onehot_local, grad_condition, (((0,), (0,)), ((), ())), precision=HIGHEST_PRECISION
    )
    grad_table = lax.psum(local_table, ("clip", "frame"))
    weight_modulate = lax.dot_general(
        cond_wide, grad_modulation, (((0,), (0,)), ((), ())), precision=HIGHEST_PRECISION
    )
    mod_by_clip = lax.psum_scatter(
        weight_modulate.astype(jnp.bfloat16), "clip", scatter_dimension=0, tiled=True
    )
    grad_modulate = lax.psum_scatter(mod_by_clip, "frame", scatter_dimension=1, tiled=True).astype(
        jnp.float32
    )
    by_clip = (
        lax.psum_scatter(
            weight_spatial_qkv.astype(jnp.bfloat16), "clip", scatter_dimension=0, tiled=True
        ).astype(jnp.float32),
        lax.psum_scatter(
            weight_spatial_out.astype(jnp.bfloat16), "clip", scatter_dimension=0, tiled=True
        ).astype(jnp.float32),
        lax.psum_scatter(
            weight_temporal_qkv.astype(jnp.bfloat16), "clip", scatter_dimension=0, tiled=True
        ).astype(jnp.float32),
        lax.psum_scatter(
            weight_temporal_out.astype(jnp.bfloat16), "clip", scatter_dimension=0, tiled=True
        ).astype(jnp.float32),
        lax.psum_scatter(
            weight_mlp_in.astype(jnp.bfloat16), "clip", scatter_dimension=0, tiled=True
        ).astype(jnp.float32),
        lax.psum_scatter(
            weight_mlp_out.astype(jnp.bfloat16), "clip", scatter_dimension=0, tiled=True
        ).astype(jnp.float32),
    )
    summed = (
        lax.psum_scatter(
            by_clip[0].astype(jnp.bfloat16), "frame", scatter_dimension=1, tiled=True
        ).astype(jnp.float32),
        lax.psum_scatter(
            by_clip[1].astype(jnp.bfloat16), "frame", scatter_dimension=1, tiled=True
        ).astype(jnp.float32),
        lax.psum_scatter(
            by_clip[2].astype(jnp.bfloat16), "frame", scatter_dimension=1, tiled=True
        ).astype(jnp.float32),
        lax.psum_scatter(
            by_clip[3].astype(jnp.bfloat16), "frame", scatter_dimension=1, tiled=True
        ).astype(jnp.float32),
        lax.psum_scatter(
            by_clip[4].astype(jnp.bfloat16), "frame", scatter_dimension=1, tiled=True
        ).astype(jnp.float32),
        lax.psum_scatter(
            by_clip[5].astype(jnp.bfloat16), "frame", scatter_dimension=1, tiled=True
        ).astype(jnp.float32),
    )
    return (
        output,
        grad_inputs,
        grad_table,
        grad_modulate,
        summed[0],
        summed[1],
        summed[2],
        summed[3],
        summed[4],
        summed[5],
    )


def solution(mesh):
    placed = (
        P("clip", "frame", None, None),
        P("clip", "frame", None, None),
        P("clip"),
        P(),
        P("clip"),
        P(),
        P(),
        P(),
        P(),
        P(),
        P(),
        P(),
        P(),
    )
    return jax.shard_map(
        local,
        mesh=mesh,
        in_specs=placed,
        out_specs=(
            P("clip", "frame", None, None),
            P("clip", "frame", None, None),
            P(),
            P("clip", "frame"),
            P("clip", "frame"),
            P("clip", "frame"),
            P("clip", "frame"),
            P("clip", "frame"),
            P("clip", "frame"),
            P("clip", "frame"),
        ),
        check_vma=False,
    )
```

profile of v0, /device:TPU:0, one launch (start us, length us, event | category | flops | bytes accessed | tf_op | source)
XLA Modules:
  0.0 1046.0 jit_solution(14938835240810155861)
XLA Ops:
  17.3 6.2 fusion.82
  31.8 7.7 convolution_convert_fusion.2
  39.5 6.7 copy.163
  46.2 8.9 reshape.1423
  60.9 3.6 exponential_reduce_fusion
  75.6 4.1 convolution_convert_fusion.1
  79.7 4.2 slice_convert_fusion.6
  86.7 6.6 collective-permute-start
  94.5 3.9 copy.172
  102.0 3.6 copy.187
  110.5 48.8 %collective-permute-done = bf16[2,4,1,256,768]{4,3,1,2,0:T(8,128)(2,1)} collective-permute-done((bf16[2,4,1,256,768]{4,3,1,2,0:T(8,128)(2,1)}, bf16[2,4,1,256,768]{4,3,1,2,0:T(8,128)(2,1)}, u32[]{:S(2)}, u32[]{:S(2)}) %collective-permute-start) | collective-permute-done | bytes 3145760 | tf_op jit(solution)/shard_map/ppermute | solution.py:24
  159.2 5.2 slice_convert_fusion.3
  168.0 3.6 copy.184
  175.1 5.2 slice_convert_fusion.2
  183.8 6.6 multiply_reduce_fusion.12
  218.3 3.7 copy.190
  225.6 10.1 fusion.47
  239.4 7.5 fusion.92
  246.9 14.8 %multiply_convert_fusion.4 = (bf16[4,1,256,768]{3,2,1,0:T(8,128)(2,1)S(1)}, f32[1024,768]{1,0:T(8,128)}) fusion(bf16[4,1,256,768]{3,2,1,0:T(8,128)(2,1)S(1)} %copy-done.25, f32[4]{0:T(128)S(1)} %copy-done.101, f32[4,768]{1,0:T(4,128)S(1)} %get-tuple-element.154, f32[4,1,256,768]{3,2,1,0:T(8,128)S(1)} %get-tuple-element.92, bf16[3072,768]{1,0:T(8,128)(2,1)} %param.29, ...), kind=kOutput, calls=%fused_computation.98 | convolution fusion | flops 4865654784 | bytes 26750992 | tf_op jit(solution)/shard_map/dot_general | solution.py:190
  261.7 15.4 %fusion.7 = bf16[1024,3072]{1,0:T(8,128)(2,1)} fusion(f32[1024,3072]{1,0:T(8,128)S(1)} %fusion.92, bf16[1024,768]{1,0:T(8,128)(2,1)S(1)} %bitcast.344, bf16[3072,768]{1,0:T(8,128)(2,1)} %param.29), kind=kOutput, calls=%fused_computation.12 | convolution fusion | flops 4894752768 | bytes 25165824 | tf_op jit(solution)/shard_map/dot_general | solution.py:54
  277.1 9.9 fusion.42
  288.9 6.8 multiply_reduce_fusion.3
  311.2 5.1 reshape.1437
  316.3 17.2 %fusion.45 = (f32[4,256,12]{1,0,2:T(4,128)S(1)}, f32[4,256,12]{1,0,2:T(4,128)S(1)}, f32[4,256,12]{1,0,2:T(4,128)S(1)}) fusion(f32[4,1,256,12,64]{2,0,4,3,1:T(4,128)} %reshape.1437, f32[4,1,256,12,64]{2,4,3,0,1:T(8,128)} %bitcast.305, f32[4,1,256,12,64]{2,4,3,0,1:T(8,128)} %bitcast.307, f32[4,1,256,12,64]{2,4,3,0,1:T(8,128)} %bitcast.303), kind=kLoop, calls=%fused_computation.83 | loop fusion | flops 4681728 | bytes 12730368 | tf_op jit(solution)/shard_map/reduce_sum | solution.py:214
  336.3 3.6 copy.193
  342.7 3.6 copy.195
  352.6 7.3 fusion.89
  362.3 12.0 %fusion.40 = (bf16[4,1,256,768]{3,2,0,1:T(8,128)(2,1)}, f32[4,1,256,768]{3,2,0,1:T(8,128)S(1)}, f32[4,1,256,768]{3,2,0,1:T(8,128)S(1)}, f32[4,1,256,768]{3,2,0,1:T(8,128)}) fusion(f32[4,1,256,768]{3,2,0,1:T(8,128)} %copy.195, f32[4,1,256,768]{3,2,0,1:T(8,128)} %copy.193, f32[4,1,256,768]{3,2,0,1:T(8,128)} %copy.194, bf16[4,1,256,2304]{3,2,0,1:T(8,128)(2,1)} %bitcast.313, ...), kind=kLoop, calls=%fused_computation.73 | loop fusion | flops 10223616 | bytes 26738688 | tf_op jit(solution)/shard_map/convert.19
  374.3 6.5 add_bitcast_fusion.1
  380.8 8.1 fusion
  389.0 6.7 fusion.86
  395.7 6.1 collective-permute-start.2
  408.8 58.2 %collective-permute-done.2 = bf16[2,4,1,256,768]{4,3,1,2,0:T(8,128)(2,1)} collective-permute-done((bf16[2,4,1,256,768]{4,3,1,2,0:T(8,128)(2,1)}, bf16[2,4,1,256,768]{4,3,1,2,0:T(8,128)(2,1)}, u32[]{:S(2)}, u32[]{:S(2)}) %collective-permute-start.2) | collective-permute-done | bytes 3145760 | tf_op jit(solution)/shard_map/ppermute | solution.py:24
  467.0 5.7 collective-permute-done.3
  472.7 5.4 fusion.11
  480.1 4.0 fusion.38
  488.4 5.9 multiply_reduce_fusion.6
  500.0 12.4 %convolution_convert_fusion.3 = bf16[3072,768]{1,0:T(8,128)(2,1)} fusion(bf16[1024,768]{1,0:T(8,128)(2,1)} %bitcast.345, f32[1024,3072]{1,0:T(8,128)} %copy-done.28), kind=kOutput, calls=%fused_computation.30 | convolution fusion | flops 4862509056 | bytes 18874368 | tf_op jit(solution)/shard_map/dot_general | solution.py:48
  512.4 9.2 convolution_convert_fusion.4
  521.7 8.5 bitcast_convert_fusion
  530.3 4.3 convolution_convert_fusion.7
  537.6 3.9 reshape.1442
  541.4 9.7 multiply_reduce_fusion
  551.2 7.5 multiply_convert_fusion
  570.7 4.5 copy.209
  579.0 5.5 convolution_convert_fusion.5
  587.4 9.7 fusion.37
  602.0 5.6 fusion.35
  608.4 10.8 %convolution_convert_fusion = bf16[768,6912]{1,0:T(8,128)(2,1)} fusion(f32[4,6912]{1,0:T(4,128)S(1)} %bitcast.340, f32[4,768]{1,0:T(4,128)S(1)} %copy-done.67), kind=kOutput, calls=%fused_computation.18 | convolution fusion | flops 260127744 | bytes 10739712 | tf_op jit(solution)/shard_map/dot_general | solution.py:302
  625.2 25.2 %reduce-scatter.37.cloned.1.call-done = bf16[96,3072]{1,0:T(8,128)(2,1)} async-done(((bf16[768,3072]{1,0:T(8,128)(2,1)}), bf16[96,3072]{1,0:T(8,128)(2,1)}) %reduce-scatter.37.cloned.1.call-update) | async-done | bytes 589840 | tf_op jit(solution)/shard_map/reduce_scatter | solution.py:324
  650.5 51.8 %reduce-scatter.33.cloned.1.call-done = bf16[96,2304]{1,0:T(8,128)(2,1)} async-done(((bf16[768,2304]{1,0:T(8,128)(2,1)}), bf16[96,2304]{1,0:T(8,128)(2,1)}) %reduce-scatter.33.cloned.1.call-update) | async-done | bytes 442384 | tf_op jit(solution)/shard_map/reduce_scatter | solution.py:318
  704.4 49.7 %reduce-scatter.29.cloned.1.call-done = bf16[96,2304]{1,0:T(8,128)(2,1)} async-done(((bf16[768,2304]{1,0:T(8,128)(2,1)}), bf16[96,2304]{1,0:T(8,128)(2,1)}) %reduce-scatter.29.cloned.1.call-update) | async-done | bytes 442384 | tf_op jit(solution)/shard_map/reduce_scatter | solution.py:312
  756.3 84.0 %reduce-scatter.27.cloned.1.call-done = bf16[96,6912]{1,0:T(8,128)(2,1)} async-done(((bf16[768,6912]{1,0:T(8,128)(2,1)}), bf16[96,6912]{1,0:T(8,128)(2,1)}) %reduce-scatter.27.cloned.1.call-update) | async-done | bytes 1327120 | tf_op jit(solution)/shard_map/reduce_scatter | solution.py:305
  843.3 7.1 fusion.61
  850.4 7.0 convolution_add_fusion.1
  869.8 5.0 fusion.34
  874.8 10.1 reduce-scatter.47.cloned.1.call-done
  887.8 21.3 %reduce-scatter.53.cloned.1.call-done = bf16[192,384]{1,0:T(8,128)(2,1)} async-done(((bf16[768,384]{1,0:T(8,128)(2,1)}), bf16[192,384]{1,0:T(8,128)(2,1)}) %reduce-scatter.53.cloned.1.call-update) | async-done | bytes 147472
  912.6 19.6 %reduce-scatter.39.cloned.1.call-done = bf16[96,768]{1,0:T(8,128)(2,1)} async-done(((bf16[96,3072]{1,0:T(8,128)(2,1)}), bf16[96,768]{1,0:T(8,128)(2,1)}) %reduce-scatter.39.cloned.1.call-update) | async-done | bytes 147472 | tf_op jit(solution)/shard_map/reduce_scatter | solution.py:344
  933.8 21.3 %reduce-scatter.49.cloned.1.call-done = bf16[576,96]{1,0:T(8,128)(2,1)} async-done(((bf16[2304,96]{1,0:T(8,128)(2,1)}), bf16[576,96]{1,0:T(8,128)(2,1)}) %reduce-scatter.49.cloned.1.call-update) | async-done | bytes 110608
  958.4 20.6 %reduce-scatter.45.cloned.1.call-done = bf16[576,96]{1,0:T(8,128)(2,1)} async-done(((bf16[2304,96]{1,0:T(8,128)(2,1)}), bf16[576,96]{1,0:T(8,128)(2,1)}) %reduce-scatter.45.cloned.1.call-update) | async-done | bytes 110608
  982.3 42.1 %reduce-scatter.43.cloned.1.call-done = bf16[1728,96]{1,0:T(8,128)(2,1)} async-done(((bf16[6912,96]{1,0:T(8,128)(2,1)}), bf16[1728,96]{1,0:T(8,128)(2,1)}) %reduce-scatter.43.cloned.1.call-update) | async-done | bytes 331792
  1028.3 6.6 all-reduce.8.cloned.1.call-done
  1034.9 3.7 copy.313
  (400 shorter events, 213.7 us)
Async XLA Ops:
  8.0 67.6 %copy-start = (bf16[768,2304]{1,0:T(8,128)(2,1)S(1)}, bf16[768,2304]{1,0:T(8,128)(2,1)}, u32[]{:S(2)}) copy-start(bf16[768,2304]{1,0:T(8,128)(2,1)} %param.26) | copy-start | bytes 10616836
  8.0 611.3 %reduce-scatter.35.cloned.1.call-start = ((), (), s32[]{:S(2)}) async-start(), calls=%async_computation.19 | async-start | bytes 1327104 | tf_op jit(solution)/shard_map/reduce_scatter | solution.py:321
  10.5 16.9 %copy-start.79 = (f32[4,256]{1,0:T(4,128)}, f32[4,256]{1,0:T(4,128)S(1)}, u32[]{:S(2)}) copy-start(f32[4,256]{1,0:T(4,128)S(1)} %broadcast_multiply_fusion.8) | copy-start | bytes 12292
  27.3 43.3 %copy-start.77 = (f32[4,1,1,1,768]{4,0,1,3,2:T(4,128)}, f32[4,1,1,1,768]{4,0,1,3,2:T(4,128)S(1)}, u32[]{:S(2)}) copy-start(f32[4,1,1,1,768]{4,0,1,3,2:T(4,128)S(1)} %copy.303) | copy-start | bytes 36868
  58.3 6.2 copy-start.19
  86.7 72.6 %collective-permute-start = (bf16[2,4,1,256,768]{4,3,1,2,0:T(8,128)(2,1)}, bf16[2,4,1,256,768]{4,3,1,2,0:T(8,128)(2,1)}, u32[]{:S(2)}, u32[]{:S(2)}) collective-permute-start(bf16[2,4,1,256,768]{4,3,1,2,0:T(8,128)(2,1)} %pad_maximum_fusion.4), channel_id=1, source_target_pairs={{0,1},{1,2},{2,3},{4,5},{5,6},{6,7},{8,9},{9,10},{10,11},{12,13},{... | collective-permute-start | bytes 9437192 | tf_op jit(solution)/shard_map/ppermute | solution.py:24
  93.2 81.9 %collective-permute-start.1 = (bf16[2,4,1,256,768]{4,3,1,2,0:T(8,128)(2,1)}, bf16[2,4,1,256,768]{4,3,1,2,0:T(8,128)(2,1)}, u32[]{:S(2)}, u32[]{:S(2)}) collective-permute-start(bf16[2,4,1,256,768]{4,3,1,2,0:T(8,128)(2,1)} %pad_maximum_fusion.4), channel_id=1, source_target_pairs={{1,0},{2,1},{3,2},{5,4},{6,5},{7,6},{9,8},{10,9},{11,10},{13,12},{... | collective-permute-start | bytes 9437192 | tf_op jit(solution)/shard_map/ppermute | solution.py:25
  191.3 9.1 copy-start.58
  225.6 10.1 copy-start.3
  225.6 10.1 copy-start.75
  237.3 9.6 copy-start.5
  239.3 7.5 copy-start.51
  239.3 7.5 copy-start.25
  239.4 7.5 copy-start.101
  246.9 14.8 %copy-start.28 = (f32[1024,3072]{1,0:T(8,128)}, f32[1024,3072]{1,0:T(8,128)S(1)}, u32[]{:S(2)}) copy-start(f32[1024,3072]{1,0:T(8,128)S(1)} %fusion.92) | copy-start | bytes 37748740
  261.7 15.4 %copy-start.44 = (bf16[4,1,256,768]{3,2,1,0:T(8,128)(2,1)}, bf16[4,1,256,768]{3,2,1,0:T(8,128)(2,1)S(1)}, u32[]{:S(2)}) copy-start(bf16[4,1,256,768]{3,2,1,0:T(8,128)(2,1)S(1)} %get-tuple-element.142) | copy-start | bytes 4718596
  288.8 6.8 copy-start.6
  288.8 7.0 copy-start.10
  288.8 7.9 copy-start.16
  288.8 8.8 copy-start.18
  288.8 9.2 copy-start.26
  288.8 9.2 copy-start.74
  288.8 9.2 copy-start.86
  288.8 9.1 copy-start.99
  288.9 9.1 copy-start.102
  316.3 17.3 %copy-start.37 = (f32[4,256,12]{1,2,0:T(8,128)S(1)}, f32[4,256,12]{1,2,0:T(8,128)}, u32[]{:S(2)}) copy-start(f32[4,256,12]{1,2,0:T(8,128)} %copy-done.36) | copy-start | bytes 147460
  316.3 17.3 %copy-start.39 = (f32[1,4,1,256,12]{3,4,1,2,0:T(8,128)S(1)}, f32[1,4,1,256,12]{3,4,1,2,0:T(8,128)}, u32[]{:S(2)}) copy-start(f32[1,4,1,256,12]{3,4,1,2,0:T(8,128)} %copy-done.38) | copy-start | bytes 147460
  316.3 17.3 %copy-start.41 = (f32[1,4,1,256,12]{3,4,1,2,0:T(8,128)S(1)}, f32[1,4,1,256,12]{3,4,1,2,0:T(8,128)}, u32[]{:S(2)}) copy-start(f32[1,4,1,256,12]{3,4,1,2,0:T(8,128)} %copy-done.40) | copy-start | bytes 147460
  316.3 17.3 %copy-start.43 = (f32[1,4,1,256,12]{3,4,1,2,0:T(8,128)S(1)}, f32[1,4,1,256,12]{3,4,1,2,0:T(8,128)}, u32[]{:S(2)}) copy-start(f32[1,4,1,256,12]{3,4,1,2,0:T(8,128)} %copy-done.42) | copy-start | bytes 147460
  316.3 17.3 %copy-start.65 = (f32[4,256,12]{1,2,0:T(8,128)S(1)}, f32[4,256,12]{1,2,0:T(8,128)}, u32[]{:S(2)}) copy-start(f32[4,256,12]{1,2,0:T(8,128)} %copy-done.64) | copy-start | bytes 147460
  362.2 18.5 %copy-start.7 = (f32[1,4,3,256,768]{4,3,1,2,0:T(8,128)}, f32[1,4,3,256,768]{4,3,1,2,0:T(8,128)S(1)}, u32[]{:S(2)}) copy-start(f32[1,4,3,256,768]{4,3,1,2,0:T(8,128)S(1)} %add_bitcast_fusion) | copy-start | bytes 28311556
  388.9 14.2 %copy-start.12 = (f32[4,1,256,768]{2,3,0,1:T(8,128)S(1)}, f32[4,1,256,768]{2,3,0,1:T(8,128)}, u32[]{:S(2)}) copy-start(f32[4,1,256,768]{2,3,0,1:T(8,128)} %copy.187) | copy-start | bytes 9437188
  388.9 14.2 %copy-start.13 = (f32[1,4,1,256,768]{3,4,1,2,0:T(8,128)S(1)}, f32[1,4,1,256,768]{3,4,1,2,0:T(8,128)}, u32[]{:S(2)}) copy-start(f32[1,4,1,256,768]{3,4,1,2,0:T(8,128)} %copy.184) | copy-start | bytes 9437188
  388.9 14.2 %copy-start.15 = (f32[1,4,1,256,768]{3,4,1,2,0:T(8,128)S(1)}, f32[1,4,1,256,768]{3,4,1,2,0:T(8,128)}, u32[]{:S(2)}) copy-start(f32[1,4,1,256,768]{3,4,1,2,0:T(8,128)} %copy.190) | copy-start | bytes 9437188
  388.9 14.2 %copy-start.59 = (f32[4,256,12]{1,2,0:T(8,128)S(1)}, f32[4,256,12]{1,2,0:T(8,128)}, u32[]{:S(2)}) copy-start(f32[4,256,12]{1,2,0:T(8,128)} %copy-done.58) | copy-start | bytes 147460
  388.9 14.2 %copy-start.61 = (f32[4,256,12]{1,2,0:T(8,128)S(1)}, f32[4,256,12]{1,2,0:T(8,128)}, u32[]{:S(2)}) copy-start(f32[4,256,12]{1,2,0:T(8,128)} %copy-done.60) | copy-start | bytes 147460
  388.9 14.2 %copy-start.63 = (f32[4,256,12]{1,2,0:T(8,128)S(1)}, f32[4,256,12]{1,2,0:T(8,128)}, u32[]{:S(2)}) copy-start(f32[4,256,12]{1,2,0:T(8,128)} %copy-done.62) | copy-start | bytes 147460
  395.7 71.3 %collective-permute-start.2 = (bf16[2,4,1,256,768]{4,3,1,2,0:T(8,128)(2,1)}, bf16[2,4,1,256,768]{4,3,1,2,0:T(8,128)(2,1)}, u32[]{:S(2)}, u32[]{:S(2)}) collective-permute-start(bf16[2,4,1,256,768]{4,3,1,2,0:T(8,128)(2,1)} %get-tuple-element.95), channel_id=1, source_target_pairs={{0,1},{1,2},{2,3},{4,5},{5,6},{6,7},{8,9},{9,10},{10,11},{12,13},{... | collective-permute-start | bytes 9437192 | tf_op jit(solution)/shard_map/ppermute | solution.py:24
  401.8 70.9 %collective-permute-start.3 = (bf16[2,4,1,256,768]{4,3,1,2,0:T(8,128)(2,1)}, bf16[2,4,1,256,768]{4,3,1,2,0:T(8,128)(2,1)}, u32[]{:S(2)}, u32[]{:S(2)}) collective-permute-start(bf16[2,4,1,256,768]{4,3,1,2,0:T(8,128)(2,1)} %get-tuple-element.96), channel_id=1, source_target_pairs={{1,0},{2,1},{3,2},{5,4},{6,5},{7,6},{9,8},{10,9},{11,10},{13,12},{... | collective-permute-start | bytes 9437192 | tf_op jit(solution)/shard_map/ppermute | solution.py:25
  408.8 212.4 %reduce-scatter.31.cloned.1.call-start = ((), (), s32[]{:S(2)}) async-start(), calls=%async_computation.17 | async-start | bytes 1327104 | tf_op jit(solution)/shard_map/reduce_scatter | solution.py:315
  488.4 7.6 copy-start.78
  499.9 123.0 %reduce-scatter.41.cloned.1.call-start = ((), (), s32[]{:S(2)}) async-start(), calls=%async_computation.22 | async-start | bytes 5308416 | tf_op jit(solution)/shard_map/reduce_scatter | solution.py:327
  512.4 138.1 %reduce-scatter.37.cloned.1.call-start = ((), (), s32[]{:S(2)}) async-start(), calls=%async_computation.20 | async-start | bytes 5308416 | tf_op jit(solution)/shard_map/reduce_scatter | solution.py:324
  521.6 180.6 %reduce-scatter.33.cloned.1.call-start = ((), (), s32[]{:S(2)}) async-start(), calls=%async_computation.18 | async-start | bytes 3981312 | tf_op jit(solution)/shard_map/reduce_scatter | solution.py:318
  530.2 223.9 %reduce-scatter.29.cloned.1.call-start = ((), (), s32[]{:S(2)}) async-start(), calls=%async_computation.16 | async-start | bytes 3981312 | tf_op jit(solution)/shard_map/reduce_scatter | solution.py:312
  541.4 9.7 copy-start.33
  551.2 7.6 copy-start.22
  584.5 255.8 %reduce-scatter.27.cloned.1.call-start = ((), (), s32[]{:S(2)}) async-start(), calls=%async_computation.15 | async-start | bytes 11943936 | tf_op jit(solution)/shard_map/reduce_scatter | solution.py:305
  601.9 5.8 copy-start.97
  601.9 5.8 copy-start.96
  601.9 6.5 copy-start.67
  619.2 244.3 %reduce-scatter.51.cloned.1.call-start = ((), (), s32[]{:S(2)}) async-start(), calls=%async_computation.27 | async-start | bytes 245760
  621.1 263.8 %reduce-scatter.47.cloned.1.call-start = ((), (), s32[]{:S(2)}) async-start(), calls=%async_computation.25 | async-start | bytes 245760
  622.9 286.2 %reduce-scatter.53.cloned.1.call-start = ((), (), s32[]{:S(2)}) async-start(), calls=%async_computation.28 | async-start | bytes 737280
  625.2 307.0 %reduce-scatter.39.cloned.1.call-start = ((), (), s32[]{:S(2)}) async-start(), calls=%async_computation.21 | async-start | bytes 737280 | tf_op jit(solution)/shard_map/reduce_scatter | solution.py:344
  650.5 304.6 %reduce-scatter.49.cloned.1.call-start = ((), (), s32[]{:S(2)}) async-start(), calls=%async_computation.26 | async-start | bytes 737280
  704.4 274.7 %reduce-scatter.45.cloned.1.call-start = ((), (), s32[]{:S(2)}) async-start(), calls=%async_computation.24 | async-start | bytes 737280
  756.2 268.3 %reduce-scatter.43.cloned.1.call-start = ((), (), s32[]{:S(2)}) async-start(), calls=%async_computation.23 | async-start | bytes 2211840
  843.0 192.0 %all-reduce.8.cloned.1.call-start = ((), (), s32[]{:S(2)}) async-start(), calls=%async_computation.14 | async-start | bytes 6144000 | tf_op jit(solution)/shard_map/psum | solution.py:301
  843.3 7.1 copy-start.35
  843.3 14.1 %slice-start.3 = ((s8[10616832]{0:T(1024)(128)(4,1)}), s8[4194304]{0:T(1024)(128)(4,1)S(1)}, s32[]{:S(2)}) async-start(s8[10616832]{0:T(1024)(128)(4,1)} %bitcast.293), calls=%async_computation.32 | async-start | bytes 8388608
  843.3 14.1 %slice-start.4 = ((s8[10616832]{0:T(1024)(128)(4,1)}), s8[4194304]{0:T(1024)(128)(4,1)S(1)}, s32[]{:S(2)}) async-start(s8[10616832]{0:T(1024)(128)(4,1)} %bitcast.293), calls=%async_computation.33 | async-start | bytes 8388608
  850.4 7.1 slice-start.5
  863.5 6.3 copy-start.70
  (69 other events, 178.7 us)
Sparse Core Ops, SparseCore 0:
  408.9 39.1 reduce-scatter.34
  500.1 35.3 reduce-scatter.30
  539.3 53.8 reduce-scatter.40
  596.6 53.8 reduce-scatter.36
  654.2 48.0 reduce-scatter.32
  706.0 48.0 reduce-scatter.28
  758.0 82.1 reduce-scatter.26
  843.2 19.3 reduce-scatter.50
  865.4 19.4 reduce-scatter.46
  887.1 21.9 reduce-scatter.52
  911.5 20.6 reduce-scatter.38
  934.4 20.6 reduce-scatter.48
  958.1 20.9 reduce-scatter.44
  981.3 43.1 reduce-scatter.42
Sparse Core Ops, SparseCore 1:
  863.6 171.2 all-reduce.7
where the time goes:
time: 1050 us
  waiting for transfers between devices  465 us (44%)
  matrix products  194 us (18%)
  local copies, waits for them, and re-layouts  191 us (18%)
  other arithmetic  162 us (15%)
  between operations  17.2 us (2%)
  starting transfers between devices  16.4 us (2%)
    unnamed x21, waiting for transfers between devices  116 us
    ppermute x2, waiting for transfers between devices, padded(): before = lax.ppermute(last, axis, up)  107 us
    reduce_scatter x1, waiting for transfers between devices, local(): lax.psum_scatter(weight_modulate.astype(jnp.bfloat16), 'clip', scatter_di...  84 us
    dot_general x9, matrix products, contract_cols(): lax.dot_general(left, right, (((1,), (1,)), ((), ())), preferred_element_...  63.3 us
    unnamed x264, local copies, waits for them, and re-layouts  63.1 us
    reduce_scatter x1, waiting for transfers between devices, local(): lax.psum_scatter(weight_temporal_qkv.astype(jnp.bfloat16), 'clip', scatte...  51.8 us
    reduce_scatter x1, waiting for transfers between devices, local(): lax.psum_scatter(weight_spatial_qkv.astype(jnp.bfloat16), 'clip', scatter...  49.7 us
    dot_general x6, matrix products, contract_rows(): lax.dot_general(left, right, (((0,), (0,)), ((), ())), preferred_element_...  40.5 us
  transfers between devices with their start and end apart: 19, of which 14 were waited for; matrix products, arithmetic and copies ran while one was open for 22% of the time, Pallas kernels for 0%

commit v1 on v0

v1 whole, which is shorter than its diff:
```python
import functools
import math

import jax
import jax.numpy as jnp
from jax import lax
from jax.experimental import pallas as pl
from jax.experimental.pallas import tpu as pltpu
from jax.sharding import PartitionSpec as P

HEAD_DIM = 64
NORM_EPSILON = 1e-06
F32 = jnp.float32
BF16 = jnp.bfloat16
LANES = 128
SLOT = 16
NO_KEY = -1e30
VMEM_LIMIT = 60 * 2**20
GELU_A = math.sqrt(2.0 / math.pi)
GELU_B = 0.044715


def dot(left, right):
    return lax.dot_general(left, right, (((1,), (0,)), ((), ())), preferred_element_type=F32)


def dot_nt(left, right):
    return lax.dot_general(left, right, (((1,), (1,)), ((), ())), preferred_element_type=F32)


def dot_tn(left, right):
    return lax.dot_general(left, right, (((0,), (0,)), ((), ())), preferred_element_type=F32)


def norm(values):
    centred = values - jnp.mean(values, axis=-1, keepdims=True)
    inv_std = lax.rsqrt(jnp.mean(centred * centred, axis=-1, keepdims=True) + NORM_EPSILON)
    return centred * inv_std, inv_std


def norm_back(grad_hidden, normed, inv_std, scale_plus):
    grad_normed = grad_hidden * scale_plus
    mean_grad = jnp.mean(grad_normed, axis=-1, keepdims=True)
    mean_cross = jnp.mean(grad_normed * normed, axis=-1, keepdims=True)
    return inv_std * (grad_normed - mean_grad - normed * mean_cross)


def column_sum(values):
    return jnp.sum(values, axis=0, keepdims=True)


def side_masks(dtype, value):
    lane = lax.broadcasted_iota(jnp.int32, (1, LANES), 1)
    return [jnp.where((lane < HEAD_DIM) == (side == 0), value, 0.0).astype(dtype) for side in (0, 1)]


def spatial_forward(
    heads, tokens, mod, posenc, w_qkv, w_out, hidden_a, qkv, mixed, branch, after, hidden_b, lse
):
    width = tokens.shape[-1]
    rows = tokens.shape[1]
    inputs = tokens[0].astype(F32)
    normed, _ = norm(inputs)
    hidden = (normed * (1.0 + mod[0, 1:2]) + mod[0, 0:1]).astype(BF16)
    hidden_a[0] = hidden
    for part in range(3):
        cols = slice(part * width, (part + 1) * width)
        qkv[0, :, cols] = dot(hidden, w_qkv[:, cols]).astype(BF16)
    masks = side_masks(BF16, HEAD_DIM**-0.5)
    lane = lax.broadcasted_iota(jnp.int32, (1, LANES), 1)
    table = jnp.zeros((rows, LANES), F32)
    for pair in range(heads // 2):
        cols = pl.ds(pair * LANES, LANES)
        query = qkv[0, :, cols]
        key = qkv[0, :, pl.ds(width + pair * LANES, LANES)]
        value = qkv[0, :, pl.ds(2 * width + pair * LANES, LANES)]
        out = []
        for side in range(2):
            scores = dot_nt(query * masks[side], key)
            top = jnp.max(scores, axis=-1, keepdims=True)
            grown = jnp.exp(scores - top)
            total = jnp.sum(grown, axis=-1, keepdims=True)
            soft = (grown * (1.0 / total)).astype(BF16)
            out.append(dot(soft, value))
            table = jnp.where(lane == 2 * pair + side, top + jnp.log(total), table)
        mixed[0, :, cols] = jnp.where(lane < HEAD_DIM, out[0], out[1]).astype(BF16)
    lse[0] = table
    branch_a = dot(mixed[0], w_out[...])
    branch[0] = branch_a.astype(BF16)
    after_a = inputs + mod[0, 2:3] * branch_a
    after[0] = after_a
    normed_b, _ = norm(after_a)
    hidden_b[0] = (normed_b * (1.0 + mod[0, 4:5]) + (mod[0, 3:4] + posenc[0])).astype(BF16)


def by_head(left, right, to_heads):
    full = left.astype(F32) * right.astype(F32)
    high = full.astype(BF16)
    rest = (full - high.astype(F32)).astype(BF16)
    return dot(high, to_heads) + dot(rest, to_heads)


def middle(
    hb_own, hb_prev, hb_next, after_a, target, mod, weight, masks, to_heads, spread, pack,
    w_qkv, w_out, w_in, w_mlp,
    output, grad_b, hidden_c, act, grad_branch_c, grad_up, mixed_b, grad_branch_b, sent, q_own,
    grad_q, sums, slope,
):
    width = after_a.shape[-1]
    ff = act.shape[-1]
    scale_qk = HEAD_DIM**-0.5
    own = hb_own[0]
    query = dot(own, w_qkv[:, :width]).astype(BF16)
    q_own[0] = query
    keys, values, scores = [], [], []
    for number, hidden in enumerate((hb_prev, hb_own, hb_next)):
        keys.append(dot(hidden[0], w_qkv[:, width : 2 * width]).astype(BF16))
        values.append(dot(hidden[0], w_qkv[:, 2 * width :]).astype(BF16))
        raw = by_head(query, keys[number], to_heads[...]) * scale_qk
        scores.append(raw + masks[number : number + 1])
    top = jnp.maximum(jnp.maximum(scores[0], scores[1]), scores[2])
    grown = [jnp.exp(entry - top) for entry in scores]
    inverse = 1.0 / (grown[0] + grown[1] + grown[2])
    soft = [entry * inverse for entry in grown]
    soft_low = [entry.astype(BF16) for entry in soft]
    to_width = spread[LANES : 2 * LANES]
    total = None
    for number in range(3):
        term = dot(soft_low[number], to_width) * values[number].astype(F32)
        total = term if total is None else total + term
    mixed = total.astype(BF16)
    mixed_b[0] = mixed
    branch_b = dot(mixed, w_out[...])
    after_b = after_a[0] + mod[0, 5:6] * branch_b
    normed_c, inv_c = norm(after_b)
    hidden = (normed_c * (1.0 + mod[0, 7:8]) + mod[0, 6:7]).astype(BF16)
    hidden_c[0] = hidden
    for part in range(ff // width):
        cols = slice(part * width, (part + 1) * width)
        upward = dot(hidden, w_in[:, cols])
        squared = upward * upward
        bent = jnp.tanh(GELU_A * upward * (1.0 + GELU_B * squared))
        act[0, :, cols] = (0.5 * upward * (1.0 + bent)).astype(BF16)
        slope[:, cols] = 0.5 * (1.0 + bent) + (0.5 * GELU_A) * upward * (1.0 - bent * bent) * (
            1.0 + 3.0 * GELU_B * squared
        )
    branch_c = dot(act[0], w_mlp[...])
    result = after_b + mod[0, 8:9] * branch_c
    output[0] = result.astype(BF16)
    grad_result = weight[0, :, :1] * (result - target[0].astype(F32))
    sums[0, 2:3] = column_sum(grad_result * branch_c)
    low_c = (mod[0, 8:9] * grad_result).astype(BF16)
    grad_branch_c[0] = low_c
    for part in range(ff // width):
        cols = slice(part * width, (part + 1) * width)
        grad_act = dot_nt(low_c, w_mlp[cols, :])
        grad_up[0, :, cols] = (grad_act * slope[:, cols]).astype(BF16)
    grad_hidden = dot_nt(grad_up[0], w_in[...])
    sums[0, 0:1] = column_sum(grad_hidden)
    sums[0, 1:2] = column_sum(grad_hidden * normed_c)
    grad_after = grad_result + norm_back(grad_hidden, normed_c, inv_c, 1.0 + mod[0, 7:8])
    grad_b[0] = grad_after
    sums[0, 3:4] = column_sum(grad_after * branch_b)
    low_b = (mod[0, 5:6] * grad_after).astype(BF16)
    grad_branch_b[0] = low_b
    grad_mixed = dot_nt(low_b, w_out[...]).astype(BF16)
    grad_soft = [by_head(grad_mixed, values[number], to_heads[...]) for number in range(3)]
    inner = soft[0] * grad_soft[0] + soft[1] * grad_soft[1] + soft[2] * grad_soft[2]
    grad_scores = [(soft[number] * (grad_soft[number] - inner)).astype(BF16) for number in range(3)]
    total = None
    for number in range(3):
        term = dot(grad_scores[number], to_width) * keys[number].astype(F32)
        total = term if total is None else total + term
    grad_q[0] = (total * scale_qk).astype(BF16)
    sent[0, :, :width] = grad_mixed
    sent[0, :, width:] = dot(
        jnp.concatenate(soft_low + grad_scores, axis=1), pack[...]
    ).astype(BF16)


def spatial_backward(
    heads, hb_prev, hb_next, sent_own, sent_prev, sent_next, q_own, grad_q, grad_b, after_a,
    tokens, branch, qkv, lse, mod, spread, w_qkv_b, w_out, w_qkv_a,
    grad_tokens, grad_qkv_b, grad_qkv_a, grad_branch_a, sums,
):
    width = after_a.shape[-1]
    scale_qk = HEAD_DIM**-0.5
    w_query = w_qkv_b[:, :width]
    queries = (
        dot(hb_prev[0], w_query).astype(BF16).astype(F32),
        q_own[0].astype(F32),
        dot(hb_next[0], w_query).astype(BF16).astype(F32),
    )
    grad_key = None
    grad_value = None
    for number, source in enumerate((sent_prev, sent_own, sent_next)):
        other = 2 - number
        table = source[0, :, width:]
        low = LANES - SLOT * other
        soft = dot(table, spread[low : low + LANES])
        low = LANES - SLOT * (3 + other)
        score = dot(table, spread[low : low + LANES])
        key_term = score * queries[number]
        value_term = soft * source[0, :, :width].astype(F32)
        grad_key = key_term if grad_key is None else grad_key + key_term
        grad_value = value_term if grad_value is None else grad_value + value_term
    grad_qkv_b[0, :, :width] = grad_q[0]
    grad_qkv_b[0, :, width : 2 * width] = (grad_key * scale_qk).astype(BF16)
    grad_qkv_b[0, :, 2 * width :] = grad_value.astype(BF16)
    grad_hidden = dot_nt(grad_qkv_b[0], w_qkv_b[...])
    normed_b, inv_b = norm(after_a[0])
    sums[0, 3:4] = column_sum(grad_hidden)
    sums[0, 4:5] = column_sum(grad_hidden * normed_b)
    grad_after = grad_b[0] + norm_back(grad_hidden, normed_b, inv_b, 1.0 + mod[0, 4:5])
    sums[0, 2:3] = column_sum(grad_after * branch[0].astype(F32))
    low_a = (mod[0, 2:3] * grad_after).astype(BF16)
    grad_branch_a[0] = low_a
    grad_mixed = dot_nt(low_a, w_out[...]).astype(BF16)
    masks = side_masks(BF16, 1.0)
    lane = lax.broadcasted_iota(jnp.int32, (1, LANES), 1)
    scale_low = jnp.asarray(scale_qk, BF16)
    for pair in range(heads // 2):
        cols = slice(pair * LANES, (pair + 1) * LANES)
        query = qkv[0, :, cols]
        key = qkv[0, :, pl.ds(width + pair * LANES, LANES)]
        value = qkv[0, :, pl.ds(2 * width + pair * LANES, LANES)]
        gm = grad_mixed[:, cols]
        parts = []
        for side in range(2):
            head = 2 * pair + side
            scores = dot_nt(query * (masks[side] * scale_low), key)
            soft = jnp.exp(scores - lse[0, :, head : head + 1])
            grad_soft = dot_nt(gm * masks[side], value)
            inner = jnp.sum(soft * grad_soft, axis=-1, keepdims=True)
            grad_scores = (soft * (grad_soft - inner)).astype(BF16)
            parts.append(
                (dot(grad_scores, key), dot_tn(grad_scores, query), dot_tn(soft.astype(BF16), gm))
            )
        for number, factor in ((0, scale_qk), (1, scale_qk), (2, 1.0)):
            both = jnp.where(lane < HEAD_DIM, parts[0][number], parts[1][number])
            start = number * width + pair * LANES
            grad_qkv_a[0, :, start : start + LANES] = (both * factor).astype(BF16)
    grad_hidden = dot_nt(grad_qkv_a[0], w_qkv_a[...])
    normed_a, inv_a = norm(tokens[0].astype(F32))
    sums[0, 0:1] = column_sum(grad_hidden)
    sums[0, 1:2] = column_sum(grad_hidden * normed_a)
    grad_tokens[0] = grad_after + norm_back(grad_hidden, normed_a, inv_a, 1.0 + mod[0, 1:2])


def weight_term(left, right, out):
    out[...] = dot_tn(left[...], right[...]).astype(BF16)


def weight_grad(left, right, tile_m, tile_n):
    rows, height = left.shape
    width = right.shape[1]
    return pl.pallas_call(
        weight_term,
        grid=(height // tile_m, width // tile_n),
        in_specs=[
            pl.BlockSpec((rows, tile_m), lambda i, j: (0, i)),
            pl.BlockSpec((rows, tile_n), lambda i, j: (0, j)),
        ],
        out_specs=pl.BlockSpec((tile_m, tile_n), lambda i, j: (i, j)),
        out_shape=jax.ShapeDtypeStruct((height, width), BF16),
        compiler_params=pltpu.CompilerParams(vmem_limit_bytes=VMEM_LIMIT),
        cost_estimate=pl.CostEstimate(
            flops=2 * rows * height * width,
            bytes_accessed=2 * (rows * height + rows * width + height * width),
            transcendentals=0,
        ),
    )(left, right)


def clip_block(array):
    rest = array.shape[1:]
    return pl.BlockSpec((1,) + rest, lambda c: (c,) + (0,) * len(rest))


def whole(array):
    return pl.BlockSpec(
        array.shape, lambda c: (0,) * array.ndim, pipeline_mode=pl.Buffered(1)
    )


def per_clip(body, blocks, wholes, outs, flops, scratch=()):
    clips = blocks[0].shape[0]
    operands = [(a, clip_block(a)) for a in blocks] + [(a, whole(a)) for a in wholes]
    touched = sum(math.prod(a.shape) * a.dtype.itemsize for a in [*blocks, *wholes, *outs])
    return pl.pallas_call(
        body,
        grid=(clips,),
        in_specs=[spec for _, spec in operands],
        out_specs=[clip_block(a) for a in outs],
        out_shape=list(outs),
        scratch_shapes=list(scratch),
        compiler_params=pltpu.CompilerParams(vmem_limit_bytes=VMEM_LIMIT),
        cost_estimate=pl.CostEstimate(flops=flops, bytes_accessed=touched, transcendentals=0),
    )(*[a for a, _ in operands])


def scatter_sum(parts, axis, bits):
    count = lax.axis_size(axis)
    me = lax.axis_index(axis)
    shape = parts.shape[1:]
    left = list(range(count.bit_length() - 1))[::-1]
    held = parts.reshape((2,) * len(left) + shape)
    for bit in bits:
        dim = left.index(bit)
        left.remove(bit)
        mine = (me >> bit) & 1
        away = lax.dynamic_index_in_dim(held, 1 - mine, dim, keepdims=False)
        keep = lax.dynamic_index_in_dim(held, mine, dim, keepdims=False)
        came = lax.ppermute(away, axis, [(i, i ^ (1 << bit)) for i in range(count)])
        total = keep.astype(F32) + came.astype(F32)
        held = total.astype(parts.dtype)
    return total.reshape(shape)


def clip_bits(first):
    bits = list(range(1, lax.axis_size("clip").bit_length() - 1))
    return [0] + (bits if first == 0 else bits[::-1])


def frame_bits():
    return list(range(lax.axis_size("frame").bit_length() - 1))


def thirds(values):
    high = values.astype(BF16)
    rest = values - high.astype(F32)
    mid = rest.astype(BF16)
    low = (rest - mid.astype(F32)).astype(BF16)
    return jnp.concatenate((high, mid, low), axis=0)


def local(
    tokens, target, loss_weight, timesteps, offsets, cond_table, modulate_w,
    spatial_qkv, spatial_out, temporal_qkv, temporal_out, mlp_in, mlp_out,
):
    clips, frames, patches, width = tokens.shape
    steps = cond_table.shape[0]
    ff = mlp_in.shape[1]
    heads = width // HEAD_DIM
    rows = clips * frames * patches
    n_clip = lax.axis_size("clip")
    n_frame = lax.axis_size("frame")
    clip_at = lax.axis_index("clip")
    frame_at = lax.axis_index("frame")
    flat = (clips, patches, width)
    tok = tokens.reshape(flat)
    tgt = target.reshape(flat)

    condition = jnp.take(cond_table, timesteps, axis=0, mode="clip")
    cond_low = jax.nn.silu(condition).astype(BF16)
    cond_here = lax.dynamic_slice_in_dim(condition, clip_at * clips, clips)
    _, silu_pull = jax.vjp(jax.nn.silu, cond_here)
    low_here = lax.dynamic_slice_in_dim(cond_low, clip_at * clips, clips)
    mod = jnp.dot(low_here, modulate_w, preferred_element_type=F32).reshape(clips, 9, width)

    half = width // 2
    positions = (offsets + frame_at).astype(F32)
    freqs = jnp.exp(jnp.arange(half, dtype=F32) * (-math.log(10000.0) / half))
    angles = positions[:, None] * freqs
    posenc = jnp.concatenate((jnp.sin(angles), jnp.cos(angles)), axis=-1)[:, None, :]

    head_of = jnp.arange(width, dtype=jnp.int32) // HEAD_DIM
    lane_ids = jnp.arange(LANES, dtype=jnp.int32)
    to_heads = (head_of[:, None] == lane_ids[None, :]).astype(BF16)
    tall = jnp.arange(2 * LANES, dtype=jnp.int32) - LANES
    spread = (tall[:, None] == head_of[None, :]).astype(BF16)
    group, inside = jnp.divmod(jnp.arange(6 * LANES, dtype=jnp.int32), LANES)
    slot_at = jnp.where(inside < heads, group * SLOT + inside, -1)
    pack = (slot_at[:, None] == lane_ids[None, :]).astype(BF16)
    side_ok = jnp.stack((frame_at > 0, frame_at >= 0, frame_at < n_frame - 1))
    masks = jnp.where(side_ok[:, None], 0.0, NO_KEY) * jnp.ones((1, LANES), F32)
    masks = jnp.pad(masks, ((0, 5), (0, 0)))
    weight = jnp.broadcast_to(loss_weight[:, None, None], (clips, 1, LANES))

    def struct(last, dtype):
        return jax.ShapeDtypeStruct((clips, patches, last), dtype)

    macs = rows * width * width
    hidden_a, qkv_a, mixed_a, branch_a, after_a, hidden_b, lse = per_clip(
        functools.partial(spatial_forward, heads),
        [tok, mod, posenc],
        [spatial_qkv, spatial_out],
        [
            struct(width, BF16), struct(3 * width, BF16), struct(width, BF16),
            struct(width, BF16), struct(width, F32), struct(width, BF16), struct(LANES, F32),
        ],
        flops=2 * macs * 7,
    )
    up = [(i, i + 1) for i in range(n_frame - 1)]
    down = [(i + 1, i) for i in range(n_frame - 1)]
    hb_prev = lax.ppermute(hidden_b, "frame", up)
    hb_next = lax.ppermute(hidden_b, "frame", down)
    (
        output, grad_b, hidden_c, act, grad_branch_c, grad_up, mixed_b, grad_branch_b, sent,
        q_own, grad_q, sums_mid,
    ) = per_clip(
        middle,
        [hidden_b, hb_prev, hb_next, after_a, tgt, mod, weight],
        [masks, to_heads, spread, pack, temporal_qkv, temporal_out, mlp_in, mlp_out],
        [
            struct(width, BF16), struct(width, F32), struct(width, BF16), struct(ff, BF16),
            struct(width, BF16), struct(ff, BF16), struct(width, BF16), struct(width, BF16),
            struct(width + LANES, BF16), struct(width, BF16), struct(width, BF16),
            jax.ShapeDtypeStruct((clips, 8, width), F32),
        ],
        flops=2 * macs * 31,
        scratch=[pltpu.VMEM((patches, ff), F32)],
    )
    sent_prev = lax.ppermute(sent, "frame", up)
    sent_next = lax.ppermute(sent, "frame", down)

    def flat_rows(array):
        return array.reshape(rows, array.shape[-1])

    weight_in = weight_grad(flat_rows(hidden_c), flat_rows(grad_up), width, width)
    weight_mlp = weight_grad(flat_rows(act), flat_rows(grad_branch_c), width, width)
    grad_tok, grad_qkv_b, grad_qkv_a, grad_branch_a, sums_back = per_clip(
        functools.partial(spatial_backward, heads),
        [
            hb_prev, hb_next, sent, sent_prev, sent_next, q_own, grad_q, grad_b, after_a,
            tok, branch_a, qkv_a, lse, mod,
        ],
        [spread, temporal_qkv, spatial_out, spatial_qkv],
        [
            struct(width, F32), struct(3 * width, BF16), struct(3 * width, BF16),
            struct(width, BF16), jax.ShapeDtypeStruct((clips, 8, width), F32),
        ],
        flops=2 * macs * 16,
    )
    weight_qkv_b = weight_grad(flat_rows(hidden_b), flat_rows(grad_qkv_b), width, width)
    weight_out_b = weight_grad(flat_rows(mixed_b), flat_rows(grad_branch_b), width, width)
    weight_qkv_a = weight_grad(flat_rows(hidden_a), flat_rows(grad_qkv_a), width, width)
    weight_out_a = weight_grad(flat_rows(mixed_a), flat_rows(grad_branch_a), width, width)

    def over_frames(by_clip):
        tall_rows, cols = by_clip.shape
        shares = by_clip.reshape(tall_rows, n_frame, cols // n_frame).transpose(1, 0, 2)
        return scatter_sum(shares.astype(BF16), "frame", frame_bits())

    def reduce_weight(term, first):
        shares = term.reshape(n_clip, term.shape[0] // n_clip, term.shape[1])
        return over_frames(scatter_sum(shares, "clip", clip_bits(first)))

    grad_mlp_in = reduce_weight(weight_in, 0)
    grad_mlp_out = reduce_weight(weight_mlp, 1)

    def reduce_pair(qkv_term, out_term):
        both = jnp.concatenate((qkv_term, out_term), axis=1)
        shares = both.reshape(n_clip, both.shape[0] // n_clip, both.shape[1])
        cut = both.shape[1] // 2
        first = scatter_sum(shares[:, :, :cut], "clip", clip_bits(0))
        second = scatter_sum(shares[:, :, cut:], "clip", clip_bits(1))
        joined = jnp.concatenate((first, second), axis=1)
        qkv_cols = qkv_term.shape[1]
        tall_rows = joined.shape[0]
        frame_shares = jnp.concatenate(
            (
                joined[:, :qkv_cols].reshape(tall_rows, n_frame, -1),
                joined[:, qkv_cols:].reshape(tall_rows, n_frame, -1),
            ),
            axis=2,
        ).transpose(1, 0, 2)
        done = scatter_sum(frame_shares.astype(BF16), "frame", frame_bits())
        return done[:, : qkv_cols // n_frame], done[:, qkv_cols // n_frame :]

    grad_temporal_qkv, grad_temporal_out = reduce_pair(weight_qkv_b, weight_out_b)
    grad_spatial_qkv, grad_spatial_out = reduce_pair(weight_qkv_a, weight_out_a)

    grad_mod = jnp.concatenate(
        (sums_back[:, :5], sums_mid[:, 3:4], sums_mid[:, :3]), axis=1
    ).reshape(clips, 9 * width)
    by_term = dot_nt(thirds(grad_mod), modulate_w).reshape(3, clips, width)
    grad_cond = silu_pull(by_term[0] + by_term[1] + by_term[2])[0]
    grad_cond = lax.psum(grad_cond, "frame")
    grad_cond = lax.all_gather(grad_cond, "clip", axis=0, tiled=True)
    onehot = (timesteps[:, None] == jnp.arange(steps, dtype=jnp.int32)[None, :]).astype(BF16)
    grad_table = dot_tn(jnp.concatenate((onehot,) * 3, axis=0), thirds(grad_cond))
    mod_cols = 9 * width // n_frame
    mod_share = scatter_sum(
        grad_mod.reshape(clips, n_frame, mod_cols).transpose(1, 0, 2), "frame", frame_bits()
    )
    mod_all = lax.all_gather(mod_share, "clip", axis=0, tiled=True)
    mod_rows = width // n_clip
    low_rows = lax.dynamic_slice_in_dim(cond_low, clip_at * mod_rows, mod_rows, axis=1)
    grad_modulate = dot_tn(jnp.concatenate((low_rows,) * 3, axis=0), thirds(mod_all))
    return (
        output.reshape(tokens.shape),
        grad_tok.reshape(tokens.shape),
        grad_table,
        grad_modulate,
        grad_spatial_qkv,
        grad_spatial_out,
        grad_temporal_qkv,
        grad_temporal_out,
        grad_mlp_in,
        grad_mlp_out,
    )


def solution(mesh):
    placed = (
        P("clip", "frame", None, None), P("clip", "frame", None, None), P("clip"), P(), P("clip"),
    ) + (P(),) * 8
    return jax.shard_map(
        local,
        mesh=mesh,
        in_specs=placed,
        out_specs=(
            P("clip", "frame", None, None), P("clip", "frame", None, None), P(),
        ) + (P("clip", "frame"),) * 7,
        check_vma=False,
    )
```

time: 1050 us -> 453 us (0.43)
  waiting for transfers between devices: 465 us -> 112 us
  matrix products: 194 us -> 15.8 us
  Pallas kernels: 0 us -> 166 us
  local copies, waits for them, and re-layouts: 191 us -> 47.8 us
  other arithmetic: 162 us -> 33.8 us
  blocking collectives: 0 us -> 35.1 us
  starting transfers between devices: 16.4 us -> 35.9 us
  between operations: 17.2 us -> 1.65 us
    reduce_scatter x8 -> x0, waiting for transfers between devices: 230 us -> none  [the longest x1 84 us: local(): lax.psum_scatter(weight_modulate.astype(jnp.bfloat16), 'clip', scatter_di...]
    dot_general x31 -> x4, matrix products: 194 us -> 15.8 us  [the longest x1 6.86 us: dot_nt(): lax.dot_general(left, right, (((1,), (1,)), ((), ())), preferred_element_...]
    pallas_call x0 -> x9, Pallas kernels: none -> 166 us  [the longest x3 123 us: per_clip(): pl.pallas_call(body, grid=(clips,), in_specs=[spec for _, spec in operand...]
    unnamed x21 -> x0, waiting for transfers between devices: 116 us -> none
    reduce_sum x19 -> x0, other arithmetic: 64 us -> none  [the longest x8 30.8 us: token_sum(): return jnp.sum(values, axis=(1, 2))]
    unnamed x264 -> x51, local copies, waits for them, and re-layouts: 63.1 us -> 6.13 us
    convert_element_type x15 -> x4, local copies, waits for them, and re-layouts: 52.6 us -> 0.61 us  [the longest x2 0.49 us: over_frames(): return scatter_sum(shares.astype(BF16), 'frame', frame_bits())]
    mul x17 -> x0, local copies, waits for them, and re-layouts: 37.9 us -> none  [the longest x6 13.3 us: local(): soft_low_b[offset_key][..., None] * value_list[offset_key]]
  transfers between devices with their start and end apart: 19 -> 32, of which waited for: 14 -> 16; matrix products, arithmetic and copies ran while one was open for 22% -> 19% of each run, Pallas kernels for 0% -> 20%
where the time goes in v1:
time: 453 us; the launch traced here: 448 us
  Pallas kernels  166 us (37%)
  waiting for transfers between devices  112 us (25%)
  local copies, waits for them, and re-layouts  47.8 us (11%)
  starting transfers between devices  35.9 us (8%)
  blocking collectives  35.1 us (8%)
  other arithmetic  33.8 us (7%)
  matrix products  15.8 us (3%)
    pallas_call x3, Pallas kernels, per_clip(): pl.pallas_call(body, grid=(clips,), in_specs=[spec for _, spec in operand...  123 us
    ppermute x28, waiting for transfers between devices, scatter_sum(): came = lax.ppermute(away, axis, [(i, i ^ 1 << bit) for i in range(count)])  78 us
    pallas_call x6, Pallas kernels, weight_grad(): pl.pallas_call(weight_term, grid=(height // tile_m, width // tile_n), in_...  42.7 us
    ppermute x1, waiting for transfers between devices, local(): hb_prev = lax.ppermute(hidden_b, 'frame', up)  29.6 us
    ppermute x28, starting transfers between devices, scatter_sum(): came = lax.ppermute(away, axis, [(i, i ^ 1 << bit) for i in range(count)])  23 us
    psum x1, blocking collectives, local(): grad_cond = lax.psum(grad_cond, 'frame')  16.6 us
    convert_element_type x16, other arithmetic, scatter_sum(): held = total.astype(parts.dtype)  13.8 us
    squeeze x25, local copies, waits for them, and re-layouts, scatter_sum(): away = lax.dynamic_index_in_dim(held, 1 - mine, dim, keepdims=False)  12.8 us
  transfers between devices with their start and end apart: 32, of which 16 were waited for; matrix products, arithmetic and copies ran while one was open for 19% of the time, Pallas kernels for 20%

profile of v1, /device:TPU:0, one launch (start us, length us, event | category | flops | bytes accessed | tf_op | source)
XLA Modules:
  0.0 447.6 jit_solution(797796209241392587)
XLA Ops:
  3.2 5.5 %fusion.59 = f32[4,6912]{1,0:T(4,128)S(1)} fusion(bf16[768,6912]{1,0:T(8,128)(2,1)} %param.19, bf16[32,768]{1,0:T(8,128)(2,1)S(1)} %multiply_convert_fusion, s32[]{:T(128)S(6)} %select_n.155), kind=kOutput, calls=%fused_computation.152 | convolution fusion | flops 42467328 | bytes 10733572 | tf_op jit(solution)/shard_map/dot_general | solution.py:359
  10.3 19.6 %shard_map.204 = (bf16[4,256,768]{2,1,0:T(8,128)(2,1)}, bf16[4,256,2304]{2,1,0:T(8,128)(2,1)}, bf16[4,256,768]{2,1,0:T(8,128)(2,1)}, bf16[4,256,768]{2,1,0:T(8,1...) custom-call(bf16[4,256,768]{2,1,0:T(8,128)(2,1)} %bitcast.234, ...), custom_call_target="tpu_custom_call" | custom-call | flops 8455716864 | bytes 21094400 | tf_op jit(solution)/shard_map/pallas_call | solution.py:290
  29.9 5.0 %collective-permute-start = (bf16[4,256,768]{2,1,0:T(8,128)(2,1)}, bf16[4,256,768]{2,1,0:T(8,128)(2,1)S(1)}, u32[]{:S(2)}, u32[]{:S(2)}) collective-permute-start(bf16[4,256,768]{2,1,0:T(8,128)(2,1)} %get-tuple-element.34.hb_own), channel_id=1, source_target_pairs={{0,1},{1,2},{2,3},{4,5},{5,6},{6,7},{8,9},{9,10},{10,11},{12,13},{... | collective-permute-start | bytes 4718600 | tf_op jit(solution)/shard_map/ppermute | solution.py:396
  34.9 1.5 collective-permute-start.1
  39.1 29.6 %collective-permute-done.hb_prev = bf16[4,256,768]{2,1,0:T(8,128)(2,1)S(1)} collective-permute-done((bf16[4,256,768]{2,1,0:T(8,128)(2,1)}, bf16[4,256,768]{2,1,0:T(8,128)(2,1)S(1)}, u32[]{:S(2)}, u32[]{:S(2)}) %collective-permute-start) | collective-permute-done | bytes 1572896 | tf_op jit(solution)/shard_map/ppermute | solution.py:396
  68.8 4.2 collective-permute-done.1.hb_next
  74.3 56.9 %shard_map.205 = (bf16[4,256,768]{2,1,0:T(8,128)(2,1)}, f32[4,256,768]{2,1,0:T(8,128)}, bf16[4,256,768]{2,1,0:T(8,128)(2,1)}, bf16[4,256,3072]{2,1,0:T(8,128)(2,...) custom-call(bf16[4,256,768]{2,1,0:T(8,128)(2,1)} %get-tuple-element., ...), custom_call_target="tpu_custom_call" | custom-call | flops 37446746112 | bytes 53168128 | tf_op jit(solution)/shard_map/pallas_call | solution.py:290
  131.2 4.7 %collective-permute-start.2 = (bf16[4,256,896]{2,1,0:T(8,128)(2,1)}, bf16[4,256,896]{2,1,0:T(8,128)(2,1)}, u32[]{:S(2)}, u32[]{:S(2)}) collective-permute-start(bf16[4,256,896]{2,1,0:T(8,128)(2,1)} %get-tuple-element.37.sent_own), channel_id=1, source_target_pairs={{0,1},{1,2},{2,3},{4,5},{5,6},{6,7},{8,9},{9,10},{10,11},{12,13},{... | collective-permute-start | bytes 5505032 | tf_op jit(solution)/shard_map/ppermute | solution.py:414
  135.8 1.7 collective-permute-start.3
  139.6 9.2 %shard_map.212 = bf16[3072,768]{1,0:T(8,128)(2,1)} custom-call(bf16[1024,3072]{1,0:T(8,128)(2,1)} %bitcast.238, bf16[1024,768]{1,0:T(8,128)(2,1)} %bitcast.248), custom_call_target="tpu_custom_call" | custom-call | flops 4831838208 | bytes 12582912 | tf_op jit(solution)/shard_map/pallas_call | solution.py:257
  148.8 4.1 constant_dynamic-slice_fusion.1
  152.9 4.3 copy.78
  157.2 2.5 copy.86
  159.7 9.2 %shard_map.211 = bf16[768,3072]{1,0:T(8,128)(2,1)} custom-call(bf16[1024,768]{1,0:T(8,128)(2,1)} %bitcast.247, bf16[1024,3072]{1,0:T(8,128)(2,1)} %bitcast.237), custom_call_target="tpu_custom_call" | custom-call | flops 4831838208 | bytes 12582912 | tf_op jit(solution)/shard_map/pallas_call | solution.py:257
  169.0 2.7 constant_dynamic-slice_fusion.3
  171.7 1.7 copy.96
  173.8 4.4 shard_map.210
  178.3 46.4 %shard_map.206 = (f32[4,256,768]{2,1,0:T(8,128)}, bf16[4,256,2304]{2,1,0:T(8,128)(2,1)}, bf16[4,256,2304]{2,1,0:T(8,128)(2,1)}, bf16[4,256,768]{2,1,0:T(8,128)(2,1)}, f32[4,8,768]{2,1,0:T(8,128)}) custom-call(bf16[4,256,768]{2,1,0:T(8,128)(2,1)} %copy-done.21, bf16[4,256,768]{2,1,0:T(8,128)(2,1)} %collective-permute-done.1.hb_next, ...), custom_call_target="tpu_custom_call" | custom-call | flops 19327352832 | bytes 49491968 | tf_op jit(solution)/shard_map/pallas_call | solution.py:290
  225.8 7.7 %shard_map.209 = bf16[768,2304]{1,0:T(8,128)(2,1)} custom-call(bf16[1024,768]{1,0:T(8,128)(2,1)} %bitcast.236, bf16[1024,2304]{1,0:T(8,128)(2,1)} %bitcast.240), custom_call_target="tpu_custom_call" | custom-call | flops 3623878656 | bytes 9830400 | tf_op jit(solution)/shard_map/pallas_call | solution.py:257
  233.5 2.9 pad_maximum_fusion.1
  237.0 1.3 dynamic-slice_bitcast_fusion.3
  238.3 1.6 dynamic-slice_bitcast_fusion.2
  239.9 7.8 %shard_map.207 = bf16[768,2304]{1,0:T(8,128)(2,1)} custom-call(bf16[1024,768]{1,0:T(8,128)(2,1)} %bitcast.244, bf16[1024,2304]{1,0:T(8,128)(2,1)} %bitcast.239), custom_call_target="tpu_custom_call" | custom-call | flops 3623878656 | bytes 9830400 | tf_op jit(solution)/shard_map/pallas_call | solution.py:257
  247.8 4.4 shard_map.208
  252.1 2.9 pad_maximum_fusion
  255.1 1.9 fusion.77
  256.9 1.5 copy-done.7
  260.0 2.6 collective-permute-start.4
  262.6 6.9 %fusion.36 = f32[12,768]{1,0:T(8,128)S(1)} fusion(bf16[768,6912]{1,0:T(8,128)(2,1)} %param.19, bf16[4,6912]{1,0:T(4,128)(2,1)S(1)} %get-tuple-element.134, bf16[4,6912]{1,0:T(4,128)(2,1)S(1)} %get-tuple-element.133, bf16[4,6912]{1,0:T(4,128)(2,1)S(1)} %convert_element_type.378), kind=kOutput, calls=%fused_computation.96 | convolution fusion | flops 127899648 | bytes 10819584 | tf_op jit(solution)/shard_map/dot_general | solution.py:28
  269.5 16.6 %psum.7 = f32[4,768]{1,0:T(4,128)S(1)} all-reduce(f32[4,768]{1,0:T(4,128)S(1)} %fusion.58), channel_id=1, replica_groups=mesh['clip'=8,'frame'=4] {'frame'}, use_global_device_ids=true, to_apply=%region_0.1 | all-reduce | flops 3072 | bytes 24576 | tf_op jit(solution)/shard_map/psum | solution.py:479
  286.1 9.2 %all-gather = f32[8,4,768]{2,1,0:T(4,128)S(1)} all-gather(f32[1,4,768]{2,1,0:T(4,128)S(1)} %bitcast.232), channel_id=1, replica_groups=mesh['clip'=8,'frame'=4] {'clip'}, dimensions={0}, use_global_device_ids=true | all-gather | bytes 110592 | tf_op jit(solution)/shard_map/all_gather | solution.py:480
  295.4 2.4 dynamic-slice_bitcast_fusion.4
  297.9 2.3 fusion.24
  300.2 2.5 collective-permute-done.5
  302.7 9.3 %all-gather.1 = f32[8,4,1728]{2,1,0:T(4,128)S(1)} all-gather(f32[1,4,1728]{2,1,0:T(4,128)S(1)} %fusion.51), channel_id=1, replica_groups=mesh['clip'=8,'frame'=4] {'clip'}, dimensions={0}, use_global_device_ids=true | all-gather | bytes 248832 | tf_op jit(solution)/shard_map/all_gather | solution.py:487
  313.6 2.9 fusion
  317.3 2.3 fusion.1
  319.8 1.6 collective-permute-start.23
  321.3 1.6 fusion.5
  323.0 1.5 collective-permute-start.15
  324.5 1.5 fusion.4
  326.8 1.6 fusion.7
  328.5 1.4 collective-permute-start.7
  330.3 15.3 %collective-permute-done.28 = bf16[2,384,768]{1,2,0:T(8,128)(2,1)S(1)} collective-permute-done((bf16[2,384,768]{1,2,0:T(8,128)(2,1)S(1)}, bf16[2,384,768]{1,2,0:T(8,128)(2,1)S(1)}, u32[]{:S(2)}, u32[]{:S(2)}) %collective-permute-start.28) | collective-permute-done | bytes 1179680 | tf_op jit(solution)/shard_map/ppermute | solution.py:314
  347.3 1.4 collective-permute-done.23
  348.7 1.5 collective-permute-start.29
  351.5 9.9 %collective-permute-done.15 = bf16[2,96,1536]{2,1,0:T(8,128)(2,1)S(1)} collective-permute-done((bf16[2,96,1536]{2,1,0:T(8,128)(2,1)S(1)}, bf16[2,96,1536]{2,1,0:T(8,128)(2,1)S(1)}, u32[]{:S(2)}, u32[]{:S(2)}) %collective-permute-start.15) | collective-permute-done | bytes 589856 | tf_op jit(solution)/shard_map/ppermute | solution.py:314
  361.3 1.5 collective-permute-start.24
  363.8 10.2 %collective-permute-done.7 = bf16[2,96,1536]{2,1,0:T(8,128)(2,1)S(1)} collective-permute-done((bf16[2,96,1536]{2,1,0:T(8,128)(2,1)S(1)}, bf16[2,96,1536]{2,1,0:T(8,128)(2,1)S(1)}, u32[]{:S(2)}, u32[]{:S(2)}) %collective-permute-start.7) | collective-permute-done | bytes 589856 | tf_op jit(solution)/shard_map/ppermute | solution.py:314
  374.0 1.5 collective-permute-start.19
  378.0 11.9 %collective-permute-done.16 = bf16[96,1536]{1,0:T(8,128)(2,1)S(1)} collective-permute-done((bf16[96,1536]{1,0:T(8,128)(2,1)S(1)}, bf16[96,1536]{1,0:T(8,128)(2,1)S(1)}, u32[]{:S(2)}, u32[]{:S(2)}) %collective-permute-start.16) | collective-permute-done | bytes 294944 | tf_op jit(solution)/shard_map/ppermute | solution.py:314
  390.4 2.0 collective-permute-done.19
  392.6 1.4 reshape.299
  394.2 1.5 maximum_bitcast_fusion.1
  401.1 1.4 reshape.289
  403.6 1.4 maximum_bitcast_fusion
  406.9 1.2 fusion.8
  410.0 1.2 fusion.9
  414.5 6.3 %collective-permute-done.12 = bf16[2,96,768]{2,1,0:T(8,128)(2,1)} collective-permute-done((bf16[2,96,768]{2,1,0:T(8,128)(2,1)}, bf16[2,96,768]{2,1,0:T(8,128)(2,1)}, u32[]{:S(2)}, u32[]{:S(2)}) %collective-permute-start.12) | collective-permute-done | bytes 294944 | tf_op jit(solution)/shard_map/ppermute | solution.py:314
  422.0 7.2 %collective-permute-done.21 = bf16[96,768]{1,0:T(8,128)(2,1)S(1)} collective-permute-done((bf16[96,768]{1,0:T(8,128)(2,1)S(1)}, bf16[96,768]{1,0:T(8,128)(2,1)S(1)}, u32[]{:S(2)}, u32[]{:S(2)}) %collective-permute-start.21) | collective-permute-done | bytes 147488 | tf_op jit(solution)/shard_map/ppermute | solution.py:314
  430.7 2.0 collective-permute-done.13
  434.3 1.6 collective-permute-start.31
  436.0 1.5 collective-permute-start.26
  437.5 7.3 %collective-permute-done.31 = bf16[384,192]{0,1:T(8,128)(2,1)S(1)} collective-permute-done((bf16[384,192]{0,1:T(8,128)(2,1)S(1)}, bf16[384,192]{0,1:T(8,128)(2,1)S(1)}, u32[]{:S(2)}, u32[]{:S(2)}) %collective-permute-start.31) | collective-permute-done | bytes 147488 | tf_op jit(solution)/shard_map/ppermute | solution.py:314
  (177 shorter events, 45.6 us)
Async XLA Ops:
  0.6 1.9 copy-start
  3.2 6.3 %copy-start.22 = (s32[4]{0:T(128)S(1)}, s32[4]{0:T(128)}, u32[]{:S(2)}) copy-start(s32[4]{0:T(128)} %param.17) | copy-start | bytes 52
  10.3 63.4 %copy-start.20 = (f32[4]{0:T(128)S(1)}, f32[4]{0:T(128)}, u32[]{:S(2)}) copy-start(f32[4]{0:T(128)} %param.15) | copy-start | bytes 52
  29.9 38.9 %collective-permute-start = (bf16[4,256,768]{2,1,0:T(8,128)(2,1)}, bf16[4,256,768]{2,1,0:T(8,128)(2,1)S(1)}, u32[]{:S(2)}, u32[]{:S(2)}) collective-permute-start(bf16[4,256,768]{2,1,0:T(8,128)(2,1)} %get-tuple-element.34.hb_own), channel_id=1, source_target_pairs={{0,1},{1,2},{2,3},{4,5},{5,6},{6,7},{8,9},{9,10},{10,11},{12,13},{... | collective-permute-start | bytes 4718600 | tf_op jit(solution)/shard_map/ppermute | solution.py:396
  34.9 38.1 %collective-permute-start.1 = (bf16[4,256,768]{2,1,0:T(8,128)(2,1)}, bf16[4,256,768]{2,1,0:T(8,128)(2,1)}, u32[]{:S(2)}, u32[]{:S(2)}) collective-permute-start(bf16[4,256,768]{2,1,0:T(8,128)(2,1)} %get-tuple-element.34.hb_own), channel_id=1, source_target_pairs={{1,0},{2,1},{3,2},{5,4},{6,5},{7,6},{9,8},{10,9},{11,10},{13,12},{... | collective-permute-start | bytes 4718600 | tf_op jit(solution)/shard_map/ppermute | solution.py:397
  68.8 5.5 %copy-start.21 = (bf16[4,256,768]{2,1,0:T(8,128)(2,1)}, bf16[4,256,768]{2,1,0:T(8,128)(2,1)S(1)}, u32[]{:S(2)}) copy-start(bf16[4,256,768]{2,1,0:T(8,128)(2,1)S(1)} %collective-permute-done.hb_prev) | copy-start | bytes 4718596
  74.3 63.3 %copy-start.19 = (s32[32]{0:T(128)S(1)}, s32[32]{0:T(128)}, u32[]{:S(2)}) copy-start(s32[32]{0:T(128)} %param.16) | copy-start | bytes 388
  131.2 47.0 %collective-permute-start.2 = (bf16[4,256,896]{2,1,0:T(8,128)(2,1)}, bf16[4,256,896]{2,1,0:T(8,128)(2,1)}, u32[]{:S(2)}, u32[]{:S(2)}) collective-permute-start(bf16[4,256,896]{2,1,0:T(8,128)(2,1)} %get-tuple-element.37.sent_own), channel_id=1, source_target_pairs={{0,1},{1,2},{2,3},{4,5},{5,6},{6,7},{8,9},{9,10},{10,11},{12,13},{... | collective-permute-start | bytes 5505032 | tf_op jit(solution)/shard_map/ppermute | solution.py:414
  135.8 42.5 %collective-permute-start.3 = (bf16[4,256,896]{2,1,0:T(8,128)(2,1)}, bf16[4,256,896]{2,1,0:T(8,128)(2,1)}, u32[]{:S(2)}, u32[]{:S(2)}) collective-permute-start(bf16[4,256,896]{2,1,0:T(8,128)(2,1)} %get-tuple-element.37.sent_own), channel_id=1, source_target_pairs={{1,0},{2,1},{3,2},{5,4},{6,5},{7,6},{9,8},{10,9},{11,10},{13,12},{... | collective-permute-start | bytes 5505032 | tf_op jit(solution)/shard_map/ppermute | solution.py:415
  157.2 156.0 %collective-permute-start.27 = (bf16[2,2,384,768]{2,3,1,0:T(8,128)(2,1)}, bf16[2,2,384,768]{2,3,1,0:T(8,128)(2,1)}, u32[]{:S(2)}, u32[]{:S(2)}) collective-permute-start(bf16[2,2,384,768]{2,3,1,0:T(8,128)(2,1)} %bitcast.217), channel_id=1, source_target_pairs={{0,4},{4,0},{8,12},{12,8},{16,20},{20,16},{24,28},{28,24},{1,5},{5... | collective-permute-start | bytes 7077896 | tf_op jit(solution)/shard_map/ppermute | solution.py:314
  173.3 143.4 %collective-permute-start.22 = (bf16[2,2,96,3072]{3,2,0,1:T(8,128)(2,1)}, bf16[2,2,96,3072]{3,2,0,1:T(8,128)(2,1)}, u32[]{:S(2)}, u32[]{:S(2)}) collective-permute-start(bf16[2,2,96,3072]{3,2,0,1:T(8,128)(2,1)} %bitcast.202), channel_id=1, source_target_pairs={{0,4},{4,0},{8,12},{12,8},{16,20},{20,16},{24,28},{28,24},{1,5},{5... | collective-permute-start | bytes 7077896 | tf_op jit(solution)/shard_map/ppermute | solution.py:314
  237.0 2.9 copy-start.2
  237.0 2.9 copy-start.5
  238.3 81.5 %collective-permute-start.14 = (bf16[2,2,96,1536]{3,2,1,0:T(8,128)(2,1)}, bf16[2,2,96,1536]{3,2,1,0:T(8,128)(2,1)}, u32[]{:S(2)}, u32[]{:S(2)}) collective-permute-start(bf16[2,2,96,1536]{3,2,1,0:T(8,128)(2,1)} %dynamic-slice_bitcast_fusion.3), channel_id=1, source_target_pairs={{0,4},{4,0},{8,12},{12,8},{16,20},{20,16},{24,28},{28,24},{1,5},{5... | collective-permute-start | bytes 3538952 | tf_op jit(solution)/shard_map/ppermute | solution.py:314
  239.9 83.1 %collective-permute-start.17 = (bf16[2,2,96,1536]{3,2,1,0:T(8,128)(2,1)}, bf16[2,2,96,1536]{3,2,1,0:T(8,128)(2,1)}, u32[]{:S(2)}, u32[]{:S(2)}) collective-permute-start(bf16[2,2,96,1536]{3,2,1,0:T(8,128)(2,1)} %dynamic-slice_bitcast_fusion.2), channel_id=1, source_target_pairs={{0,4},{4,0},{8,12},{12,8},{16,20},{20,16},{24,28},{28,24},{1,5},{5... | collective-permute-start | bytes 3538952 | tf_op jit(solution)/shard_map/ppermute | solution.py:314
  256.9 1.5 copy-start.7
  260.0 37.8 %collective-permute-start.4 = (f32[2,4,1728]{2,1,0:T(4,128)S(1)}, f32[2,4,1728]{2,1,0:T(4,128)S(1)}, u32[]{:S(2)}, u32[]{:S(2)}) collective-permute-start(f32[2,4,1728]{2,1,0:T(4,128)S(1)} %bitcast.231), channel_id=1, source_target_pairs={{0,1},{1,0},{2,3},{3,2},{4,5},{5,4},{6,7},{7,6},{8,9},{9,8},{10,11... | collective-permute-start | bytes 165896 | tf_op jit(solution)/shard_map/ppermute | solution.py:314
  297.9 4.8 %collective-permute-start.5 = (f32[4,1728]{1,0:T(4,128)S(1)}, f32[4,1728]{1,0:T(4,128)S(1)}, u32[]{:S(2)}, u32[]{:S(2)}) collective-permute-start(f32[4,1728]{1,0:T(4,128)S(1)} %dynamic-slice_bitcast_fusion.24), channel_id=1, source_target_pairs={{0,2},{1,3},{2,0},{3,1},{4,6},{5,7},{6,4},{7,5},{8,10},{9,11},{10,... | collective-permute-start | bytes 82952 | tf_op jit(solution)/shard_map/ppermute | solution.py:314
  302.7 23.4 %collective-permute-start.6 = (bf16[2,2,96,1536]{3,2,1,0:T(8,128)(2,1)}, bf16[2,2,96,1536]{3,2,1,0:T(8,128)(2,1)}, u32[]{:S(2)}, u32[]{:S(2)}) collective-permute-start(bf16[2,2,96,1536]{3,2,1,0:T(8,128)(2,1)} %dynamic-slice_bitcast_fusion.5), channel_id=1, source_target_pairs={{0,4},{4,0},{8,12},{12,8},{16,20},{20,16},{24,28},{28,24},{1,5},{5... | collective-permute-start | bytes 3538952 | tf_op jit(solution)/shard_map/ppermute | solution.py:314
  313.3 15.2 %collective-permute-start.9 = (bf16[2,2,96,1536]{3,2,1,0:T(8,128)(2,1)}, bf16[2,2,96,1536]{3,2,1,0:T(8,128)(2,1)S(1)}, u32[]{:S(2)}, u32[]{:S(2)}) collective-permute-start(bf16[2,2,96,1536]{3,2,1,0:T(8,128)(2,1)} %dynamic-slice_bitcast_fusion.4), channel_id=1, source_target_pairs={{0,4},{4,0},{8,12},{12,8},{16,20},{20,16},{24,28},{28,24},{1,5},{5... | collective-permute-start | bytes 3538952 | tf_op jit(solution)/shard_map/ppermute | solution.py:314
  316.7 28.9 %collective-permute-start.28 = (bf16[2,384,768]{1,2,0:T(8,128)(2,1)S(1)}, bf16[2,384,768]{1,2,0:T(8,128)(2,1)S(1)}, u32[]{:S(2)}, u32[]{:S(2)}) collective-permute-start(bf16[2,384,768]{1,2,0:T(8,128)(2,1)S(1)} %dynamic-slice_bitcast_fusion), channel_id=1, source_target_pairs={{0,16},{4,20},{8,24},{12,28},{16,0},{20,4},{24,8},{28,12},{1,17},{... | collective-permute-start | bytes 3538952 | tf_op jit(solution)/shard_map/ppermute | solution.py:314
  319.6 1.7 copy-start.6
  319.8 4.8 %copy-start.3 = (bf16[8,96,1536]{2,1,0:T(8,128)(2,1)S(1)}, bf16[8,96,1536]{2,1,0:T(8,128)(2,1)}, u32[]{:S(2)}) copy-start(bf16[8,96,1536]{2,1,0:T(8,128)(2,1)} %copy-done.2) | copy-start | bytes 7077892
  319.8 28.9 %collective-permute-start.23 = (bf16[2,96,3072]{2,1,0:T(8,128)(2,1)S(1)}, bf16[2,96,3072]{2,1,0:T(8,128)(2,1)S(1)}, u32[]{:S(2)}, u32[]{:S(2)}) collective-permute-start(bf16[2,96,3072]{2,1,0:T(8,128)(2,1)S(1)} %dynamic-slice_bitcast_fusion.1), channel_id=1, source_target_pairs={{0,8},{4,12},{8,0},{12,4},{16,24},{20,28},{24,16},{28,20},{1,9},{5... | collective-permute-start | bytes 3538952 | tf_op jit(solution)/shard_map/ppermute | solution.py:314
  322.9 3.9 copy-start.8
  323.0 38.4 %collective-permute-start.15 = (bf16[2,96,1536]{2,1,0:T(8,128)(2,1)S(1)}, bf16[2,96,1536]{2,1,0:T(8,128)(2,1)S(1)}, u32[]{:S(2)}, u32[]{:S(2)}) collective-permute-start(bf16[2,96,1536]{2,1,0:T(8,128)(2,1)S(1)} %dynamic-slice_bitcast_fusion.9), channel_id=1, source_target_pairs={{0,8},{4,12},{8,0},{12,4},{16,24},{20,28},{24,16},{28,20},{1,9},{5... | collective-permute-start | bytes 1769480 | tf_op jit(solution)/shard_map/ppermute | solution.py:314
  326.1 3.8 copy-start.4
  326.1 36.9 %collective-permute-start.18 = (bf16[2,96,1536]{2,1,0:T(8,128)(2,1)S(1)}, bf16[2,96,1536]{2,1,0:T(8,128)(2,1)S(1)}, u32[]{:S(2)}, u32[]{:S(2)}) collective-permute-start(bf16[2,96,1536]{2,1,0:T(8,128)(2,1)S(1)} %dynamic-slice_bitcast_fusion.8), channel_id=1, source_target_pairs={{0,16},{4,20},{8,24},{12,28},{16,0},{20,4},{24,8},{28,12},{1,17},{... | collective-permute-start | bytes 1769480 | tf_op jit(solution)/shard_map/ppermute | solution.py:314
  328.5 45.5 %collective-permute-start.7 = (bf16[2,96,1536]{2,1,0:T(8,128)(2,1)S(1)}, bf16[2,96,1536]{2,1,0:T(8,128)(2,1)S(1)}, u32[]{:S(2)}, u32[]{:S(2)}) collective-permute-start(bf16[2,96,1536]{2,1,0:T(8,128)(2,1)S(1)} %dynamic-slice_bitcast_fusion.11), channel_id=1, source_target_pairs={{0,8},{4,12},{8,0},{12,4},{16,24},{20,28},{24,16},{28,20},{1,9},{5... | collective-permute-start | bytes 1769480 | tf_op jit(solution)/shard_map/ppermute | solution.py:314
  345.6 30.8 %collective-permute-start.10 = (bf16[2,96,1536]{2,1,0:T(8,128)(2,1)S(1)}, bf16[2,96,1536]{2,1,0:T(8,128)(2,1)S(1)}, u32[]{:S(2)}, u32[]{:S(2)}) collective-permute-start(bf16[2,96,1536]{2,1,0:T(8,128)(2,1)S(1)} %dynamic-slice_bitcast_fusion.10), channel_id=1, source_target_pairs={{0,16},{4,20},{8,24},{12,28},{16,0},{20,4},{24,8},{28,12},{1,17},{... | collective-permute-start | bytes 1769480 | tf_op jit(solution)/shard_map/ppermute | solution.py:314
  348.7 58.3 %collective-permute-start.29 = (bf16[384,768]{0,1:T(8,128)(2,1)}, bf16[384,768]{0,1:T(8,128)(2,1)}, u32[]{:S(2)}, u32[]{:S(2)}) collective-permute-start(bf16[384,768]{0,1:T(8,128)(2,1)} %dynamic-slice_bitcast_fusion.6), channel_id=1, source_target_pairs={{0,8},{4,12},{8,0},{12,4},{16,24},{20,28},{24,16},{28,20},{1,9},{5... | collective-permute-start | bytes 1769480 | tf_op jit(solution)/shard_map/ppermute | solution.py:314
  361.3 48.7 %collective-permute-start.24 = (bf16[96,3072]{1,0:T(8,128)(2,1)}, bf16[96,3072]{1,0:T(8,128)(2,1)}, u32[]{:S(2)}, u32[]{:S(2)}) collective-permute-start(bf16[96,3072]{1,0:T(8,128)(2,1)} %dynamic-slice_bitcast_fusion.7), channel_id=1, source_target_pairs={{0,16},{4,20},{8,24},{12,28},{16,0},{20,4},{24,8},{28,12},{1,17},{... | collective-permute-start | bytes 1769480 | tf_op jit(solution)/shard_map/ppermute | solution.py:314
  363.0 26.8 %collective-permute-start.16 = (bf16[96,1536]{1,0:T(8,128)(2,1)S(1)}, bf16[96,1536]{1,0:T(8,128)(2,1)S(1)}, u32[]{:S(2)}, u32[]{:S(2)}) collective-permute-start(bf16[96,1536]{1,0:T(8,128)(2,1)S(1)} %dynamic-slice_bitcast_fusion.16), channel_id=1, source_target_pairs={{0,16},{4,20},{8,24},{12,28},{16,0},{20,4},{24,8},{28,12},{1,17},{... | collective-permute-start | bytes 884744 | tf_op jit(solution)/shard_map/ppermute | solution.py:314
  374.0 18.4 %collective-permute-start.19 = (bf16[96,1536]{1,0:T(8,128)(2,1)S(1)}, bf16[96,1536]{1,0:T(8,128)(2,1)S(1)}, u32[]{:S(2)}, u32[]{:S(2)}) collective-permute-start(bf16[96,1536]{1,0:T(8,128)(2,1)S(1)} %dynamic-slice_bitcast_fusion.15), channel_id=1, source_target_pairs={{0,8},{4,12},{8,0},{12,4},{16,24},{20,28},{24,16},{28,20},{1,9},{5... | collective-permute-start | bytes 884744 | tf_op jit(solution)/shard_map/ppermute | solution.py:314
  375.6 16.9 %copy-start.15 = (bf16[2,96,1536]{2,1,0:T(8,128)(2,1)}, bf16[2,96,1536]{2,1,0:T(8,128)(2,1)S(1)}, u32[]{:S(2)}) copy-start(bf16[2,96,1536]{2,1,0:T(8,128)(2,1)S(1)} %fusion.13) | copy-start | bytes 1769476
  376.4 23.6 %collective-permute-start.8 = (bf16[96,1536]{1,0:T(8,128)(2,1)}, bf16[96,1536]{1,0:T(8,128)(2,1)}, u32[]{:S(2)}, u32[]{:S(2)}) collective-permute-start(bf16[96,1536]{1,0:T(8,128)(2,1)} %dynamic-slice_bitcast_fusion.19), channel_id=1, source_target_pairs={{0,16},{4,20},{8,24},{12,28},{16,0},{20,4},{24,8},{28,12},{1,17},{... | collective-permute-start | bytes 884744 | tf_op jit(solution)/shard_map/ppermute | solution.py:314
  377.1 15.4 %copy-start.17 = (bf16[2,96,1536]{2,1,0:T(8,128)(2,1)}, bf16[2,96,1536]{2,1,0:T(8,128)(2,1)S(1)}, u32[]{:S(2)}) copy-start(bf16[2,96,1536]{2,1,0:T(8,128)(2,1)S(1)} %fusion.12) | copy-start | bytes 1769476
  389.8 8.4 %collective-permute-start.11 = (bf16[96,1536]{1,0:T(8,128)(2,1)}, bf16[96,1536]{1,0:T(8,128)(2,1)}, u32[]{:S(2)}, u32[]{:S(2)}) collective-permute-start(bf16[96,1536]{1,0:T(8,128)(2,1)} %dynamic-slice_bitcast_fusion.18), channel_id=1, source_target_pairs={{0,8},{4,12},{8,0},{12,4},{16,24},{20,28},{24,16},{28,20},{1,9},{5... | collective-permute-start | bytes 884744 | tf_op jit(solution)/shard_map/ppermute | solution.py:314
  394.1 4.1 copy-start.18
  394.2 5.8 %copy-start.16 = (bf16[2,96,1536]{2,1,0:T(8,128)(2,1)S(1)}, bf16[2,96,1536]{2,1,0:T(8,128)(2,1)}, u32[]{:S(2)}) copy-start(bf16[2,96,1536]{2,1,0:T(8,128)(2,1)} %copy-done.15) | copy-start | bytes 1769476
  395.7 0.8 copy-start.9
  397.3 15.6 %collective-permute-start.20 = (bf16[2,96,768]{2,1,0:T(8,128)(2,1)}, bf16[2,96,768]{2,1,0:T(8,128)(2,1)}, u32[]{:S(2)}, u32[]{:S(2)}) collective-permute-start(bf16[2,96,768]{2,1,0:T(8,128)(2,1)} %dynamic-slice_bitcast_fusion.14), channel_id=1, source_target_pairs={{0,1},{1,0},{2,3},{3,2},{4,5},{5,4},{6,7},{7,6},{8,9},{9,8},{10,11... | collective-permute-start | bytes 884744 | tf_op jit(solution)/shard_map/ppermute | solution.py:314
  405.0 3.1 copy-start.11
  405.9 15.0 %collective-permute-start.12 = (bf16[2,96,768]{2,1,0:T(8,128)(2,1)}, bf16[2,96,768]{2,1,0:T(8,128)(2,1)}, u32[]{:S(2)}, u32[]{:S(2)}) collective-permute-start(bf16[2,96,768]{2,1,0:T(8,128)(2,1)} %dynamic-slice_bitcast_fusion.17), channel_id=1, source_target_pairs={{0,1},{1,0},{2,3},{3,2},{4,5},{5,4},{6,7},{7,6},{8,9},{9,8},{10,11... | collective-permute-start | bytes 884744 | tf_op jit(solution)/shard_map/ppermute | solution.py:314
  408.2 3.6 copy-start.13
  409.0 3.9 copy-start.10
  409.0 25.1 %collective-permute-start.30 = (bf16[2,384,192]{1,2,0:T(8,128)(2,1)}, bf16[2,384,192]{1,2,0:T(8,128)(2,1)S(1)}, u32[]{:S(2)}, u32[]{:S(2)}) collective-permute-start(bf16[2,384,192]{1,2,0:T(8,128)(2,1)} %dynamic-slice_bitcast_fusion.12), channel_id=1, source_target_pairs={{0,1},{1,0},{2,3},{3,2},{4,5},{5,4},{6,7},{7,6},{8,9},{9,8},{10,11... | collective-permute-start | bytes 884744 | tf_op jit(solution)/shard_map/ppermute | solution.py:314
  411.2 9.7 %copy-start.12 = (bf16[4,96,768]{2,1,0:T(8,128)(2,1)S(1)}, bf16[4,96,768]{2,1,0:T(8,128)(2,1)}, u32[]{:S(2)}) copy-start(bf16[4,96,768]{2,1,0:T(8,128)(2,1)} %copy-done.11) | copy-start | bytes 1769476
  411.8 22.4 %copy-start.14 = (bf16[384,768]{0,1:T(8,128)(2,1)S(1)}, bf16[384,768]{0,1:T(8,128)(2,1)}, u32[]{:S(2)}) copy-start(bf16[384,768]{0,1:T(8,128)(2,1)} %copy-done.13) | copy-start | bytes 1769476
  411.8 24.1 %collective-permute-start.25 = (bf16[2,96,768]{2,1,0:T(8,128)(2,1)S(1)}, bf16[2,96,768]{2,1,0:T(8,128)(2,1)S(1)}, u32[]{:S(2)}, u32[]{:S(2)}) collective-permute-start(bf16[2,96,768]{2,1,0:T(8,128)(2,1)S(1)} %dynamic-slice_bitcast_fusion.13), channel_id=1, source_target_pairs={{0,1},{1,0},{2,3},{3,2},{4,5},{5,4},{6,7},{7,6},{8,9},{9,8},{10,11... | collective-permute-start | bytes 884744 | tf_op jit(solution)/shard_map/ppermute | solution.py:314
  414.0 15.2 %collective-permute-start.21 = (bf16[96,768]{1,0:T(8,128)(2,1)S(1)}, bf16[96,768]{1,0:T(8,128)(2,1)S(1)}, u32[]{:S(2)}, u32[]{:S(2)}) collective-permute-start(bf16[96,768]{1,0:T(8,128)(2,1)S(1)} %dynamic-slice_bitcast_fusion.22), channel_id=1, source_target_pairs={{0,2},{1,3},{2,0},{3,1},{4,6},{5,7},{6,4},{7,5},{8,10},{9,11},{10,... | collective-permute-start | bytes 442376 | tf_op jit(solution)/shard_map/ppermute | solution.py:314
  421.9 10.7 %collective-permute-start.13 = (bf16[96,768]{1,0:T(8,128)(2,1)S(1)}, bf16[96,768]{1,0:T(8,128)(2,1)S(1)}, u32[]{:S(2)}, u32[]{:S(2)}) collective-permute-start(bf16[96,768]{1,0:T(8,128)(2,1)S(1)} %dynamic-slice_bitcast_fusion.23), channel_id=1, source_target_pairs={{0,2},{1,3},{2,0},{3,1},{4,6},{5,7},{6,4},{7,5},{8,10},{9,11},{10,... | collective-permute-start | bytes 442376 | tf_op jit(solution)/shard_map/ppermute | solution.py:314
  430.0 17.5 %copy-start.1 = (f32[1000,768]{1,0:T(8,128)S(1)}, f32[1000,768]{1,0:T(8,128)}, u32[]{:S(2)}) copy-start(f32[1000,768]{1,0:T(8,128)} %param.18) | copy-start | bytes 9216004
  434.3 10.5 %collective-permute-start.31 = (bf16[384,192]{0,1:T(8,128)(2,1)S(1)}, bf16[384,192]{0,1:T(8,128)(2,1)S(1)}, u32[]{:S(2)}, u32[]{:S(2)}) collective-permute-start(bf16[384,192]{0,1:T(8,128)(2,1)S(1)} %dynamic-slice_bitcast_fusion.20), channel_id=1, source_target_pairs={{0,2},{1,3},{2,0},{3,1},{4,6},{5,7},{6,4},{7,5},{8,10},{9,11},{10,... | collective-permute-start | bytes 442376 | tf_op jit(solution)/shard_map/ppermute | solution.py:314
  436.0 10.7 %collective-permute-start.26 = (bf16[96,768]{1,0:T(8,128)(2,1)S(1)}, bf16[96,768]{1,0:T(8,128)(2,1)S(1)}, u32[]{:S(2)}, u32[]{:S(2)}) collective-permute-start(bf16[96,768]{1,0:T(8,128)(2,1)S(1)} %dynamic-slice_bitcast_fusion.21), channel_id=1, source_target_pairs={{0,2},{1,3},{2,0},{3,1},{4,6},{5,7},{6,4},{7,5},{8,10},{9,11},{10,... | collective-permute-start | bytes 442376 | tf_op jit(solution)/shard_map/ppermute | solution.py:314

commit v2 on v1

--- a/solution.py
+++ b/solution.py
@@ -55,8 +55,47 @@
 
 
 def spatial_forward(
-    heads, tokens, mod, posenc, w_qkv, w_out, hidden_a, qkv, mixed, branch, after, hidden_b, lse
+    heads, tokens, mod, posenc, w_qkv, w_out, hidden_a, qkv, mixed, branch, after, hidden_b, lse,
+    from_prev, from_next, held, blank, send_sems, recv_sems, blank_sems,
 ):
+    clip = pl.program_id(0)
+    clips = pl.num_programs(0)
+    me = lax.axis_index("frame")
+    count = lax.axis_size("frame")
+    has_prev = me > 0
+    has_next = me < count - 1
+    barrier = pltpu.get_barrier_semaphore()
+
+    def move(way, number):
+        return pltpu.make_async_remote_copy(
+            src_ref=held.at[number],
+            dst_ref=(from_prev, from_next)[way].at[number],
+            send_sem=send_sems.at[way, number],
+            recv_sem=recv_sems.at[way, number],
+            device_id={"frame": me + 1 if way == 0 else me - 1},
+            device_id_type=pl.DeviceIdType.MESH,
+        )
+
+    def fill(way, number):
+        return pltpu.make_async_copy(
+            blank, (from_prev, from_next)[way].at[number], blank_sems.at[number]
+        )
+
+    @pl.when(clip == 0)
+    def _():
+        blank[...] = jnp.zeros_like(blank)
+
+        @pl.when(has_prev)
+        def _():
+            pl.semaphore_signal(
+                barrier, inc=1, device_id={"frame": me - 1}, device_id_type=pl.DeviceIdType.MESH
+            )
+
+        @pl.when(has_next)
+        def _():
+            pl.semaphore_signal(
+                barrier, inc=1, device_id={"frame": me + 1}, device_id_type=pl.DeviceIdType.MESH
+            )
     width = tokens.shape[-1]
     rows = tokens.shape[1]
     inputs = tokens[0].astype(F32)
@@ -90,7 +129,51 @@
     after_a = inputs + mod[0, 2:3] * branch_a
     after[0] = after_a
     normed_b, _ = norm(after_a)
-    hidden_b[0] = (normed_b * (1.0 + mod[0, 4:5]) + (mod[0, 3:4] + posenc[0])).astype(BF16)
+    hidden = (normed_b * (1.0 + mod[0, 4:5]) + (mod[0, 3:4] + posenc[0])).astype(BF16)
+    hidden_b[0] = hidden
+    held[clip] = hidden
+
+    @pl.when(clip == 0)
+    def _():
+        pl.semaphore_wait(barrier, jnp.where(has_prev, 1, 0) + jnp.where(has_next, 1, 0))
+
+    @pl.when(has_next)
+    def _():
+        move(0, clip).start()
+
+    @pl.when(has_prev)
+    def _():
+        move(1, clip).start()
+
+    @pl.when(jnp.logical_not(has_prev))
+    def _():
+        fill(0, clip).start()
+
+    @pl.when(jnp.logical_not(has_next))
+    def _():
+        fill(1, clip).start()
+
+    @pl.when(clip == clips - 1)
+    def _():
+        for number in range(held.shape[0]):
+
+            @pl.when(has_next)
+            def _():
+                move(0, number).wait_send()
+                move(1, number).wait_recv()
+
+            @pl.when(has_prev)
+            def _():
+                move(1, number).wait_send()
+                move(0, number).wait_recv()
+
+            @pl.when(jnp.logical_not(has_prev))
+            def _():
+                fill(0, number).wait()
+
+            @pl.when(jnp.logical_not(has_next))
+            def _():
+                fill(1, number).wait()
 
 
 def by_head(left, right, to_heads):
@@ -283,7 +366,7 @@
     )
 
 
-def per_clip(body, blocks, wholes, outs, flops, scratch=()):
+def per_clip(body, blocks, wholes, outs, flops, scratch=(), landing=()):
     clips = blocks[0].shape[0]
     operands = [(a, clip_block(a)) for a in blocks] + [(a, whole(a)) for a in wholes]
     touched = sum(math.prod(a.shape) * a.dtype.itemsize for a in [*blocks, *wholes, *outs])
@@ -291,10 +374,13 @@
         body,
         grid=(clips,),
         in_specs=[spec for _, spec in operands],
-        out_specs=[clip_block(a) for a in outs],
-        out_shape=list(outs),
+        out_specs=[clip_block(a) for a in outs] + [pl.BlockSpec(memory_space=pl.ANY)] * len(landing),
+        out_shape=[*outs, *landing],
         scratch_shapes=list(scratch),
-        compiler_params=pltpu.CompilerParams(vmem_limit_bytes=VMEM_LIMIT),
+        compiler_params=pltpu.CompilerParams(
+            vmem_limit_bytes=VMEM_LIMIT,
+            **({"collective_id": 1, "has_side_effects": True} if landing else {}),
+        ),
         cost_estimate=pl.CostEstimate(flops=flops, bytes_accessed=touched, transcendentals=0),
     )(*[a for a, _ in operands])
 
@@ -381,7 +467,7 @@
         return jax.ShapeDtypeStruct((clips, patches, last), dtype)
 
     macs = rows * width * width
-    hidden_a, qkv_a, mixed_a, branch_a, after_a, hidden_b, lse = per_clip(
+    hidden_a, qkv_a, mixed_a, branch_a, after_a, hidden_b, lse, hb_prev, hb_next = per_clip(
         functools.partial(spatial_forward, heads),
         [tok, mod, posenc],
         [spatial_qkv, spatial_out],
@@ -390,11 +476,15 @@
             struct(width, BF16), struct(width, F32), struct(width, BF16), struct(LANES, F32),
         ],
         flops=2 * macs * 7,
+        scratch=[
+            pltpu.VMEM(flat, BF16), pltpu.VMEM((patches, width), BF16),
+            pltpu.SemaphoreType.DMA((2, clips)), pltpu.SemaphoreType.DMA((2, clips)),
+            pltpu.SemaphoreType.DMA((clips,)),
+        ],
+        landing=[struct(width, BF16)] * 2,
     )
     up = [(i, i + 1) for i in range(n_frame - 1)]
     down = [(i + 1, i) for i in range(n_frame - 1)]
-    hb_prev = lax.ppermute(hidden_b, "frame", up)
-    hb_next = lax.ppermute(hidden_b, "frame", down)
     (
         output, grad_b, hidden_c, act, grad_branch_c, grad_up, mixed_b, grad_branch_b, sent,
         q_own, grad_q, sums_mid,

time: 453 us -> 438 us (0.967)
  waiting for transfers between devices: 112 us -> 80.6 us
  Pallas kernels: 166 us -> 193 us
  starting transfers between devices: 35.9 us -> 26.8 us
    ppermute x2 -> x0, waiting for transfers between devices: 33.8 us -> none  [the longest x1 29.6 us: local(): hb_prev = lax.ppermute(hidden_b, 'frame', up)]
    pallas_call x3, Pallas kernels: 123 us -> 149 us  [per_clip(): pl.pallas_call(body, grid=(clips,), in_specs=[spec for _, spec in operand...]
    ppermute x2 -> x0, starting transfers between devices: 6.52 us -> none  [the longest x1 5.01 us: local(): hb_prev = lax.ppermute(hidden_b, 'frame', up)]
  transfers between devices with their start and end apart: 32 -> 30, of which waited for: 16 -> 14; matrix products, arithmetic and copies ran while one was open for 19% -> 18% of each run, Pallas kernels for 20% -> 21%
where the time goes in v2:
time: 438 us; the launch traced here: 433 us
  Pallas kernels  193 us (44%)
  waiting for transfers between devices  80.6 us (18%)
  local copies, waits for them, and re-layouts  45.9 us (10%)
  blocking collectives  35.5 us (8%)
  other arithmetic  33.8 us (8%)
  starting transfers between devices  26.8 us (6%)
  matrix products  15.8 us (4%)
    pallas_call x3, Pallas kernels, per_clip(): pl.pallas_call(body, grid=(clips,), in_specs=[spec for _, spec in operand...  149 us
    ppermute x28, waiting for transfers between devices, scatter_sum(): came = lax.ppermute(away, axis, [(i, i ^ 1 << bit) for i in range(count)])  78 us
    pallas_call x6, Pallas kernels, weight_grad(): pl.pallas_call(weight_term, grid=(height // tile_m, width // tile_n), in_...  43.2 us
    ppermute x28, starting transfers between devices, scatter_sum(): came = lax.ppermute(away, axis, [(i, i ^ 1 << bit) for i in range(count)])  20.8 us
    psum x1, blocking collectives, local(): grad_cond = lax.psum(grad_cond, 'frame')  17 us
    convert_element_type x16, other arithmetic, scatter_sum(): held = total.astype(parts.dtype)  13.8 us
    squeeze x25, local copies, waits for them, and re-layouts, scatter_sum(): away = lax.dynamic_index_in_dim(held, 1 - mine, dim, keepdims=False)  12.8 us
    all_gather x1, blocking collectives, local(): mod_all = lax.all_gather(mod_share, 'clip', axis=0, tiled=True)  9.27 us
  transfers between devices with their start and end apart: 30, of which 14 were waited for; matrix products, arithmetic and copies ran while one was open for 18% of the time, Pallas kernels for 21%

profile of v2, /device:TPU:0, one launch (start us, length us, event | category | flops | bytes accessed | tf_op | source)
XLA Modules:
  0.0 432.6 jit_solution(13033730347848017010)
XLA Ops:
  3.2 5.5 %fusion.59 = f32[4,6912]{1,0:T(4,128)S(1)} fusion(bf16[768,6912]{1,0:T(8,128)(2,1)} %param.19, bf16[32,768]{1,0:T(8,128)(2,1)S(1)} %multiply_convert_fusion, s32[]{:T(128)S(6)} %select_n.155), kind=kOutput, calls=%fused_computation.152 | convolution fusion | flops 42467328 | bytes 10733572 | tf_op jit(solution)/shard_map/dot_general | solution.py:445
  12.9 46.0 %shard_map.204 = (bf16[4,256,768]{2,1,0:T(8,128)(2,1)}, bf16[4,256,2304]{2,1,0:T(8,128)(2,1)}, bf16[4,256,768]{2,1,0:T(8,128)(2,1)}, bf16[4,256,768]{2,1,0:T(8,1...) custom-call(bf16[4,256,768]{2,1,0:T(8,128)(2,1)} %bitcast.234, ...), custom_call_target="tpu_custom_call" | custom-call | flops 8455716864 | bytes 21094400 | tf_op jit(solution)/shard_map/pallas_call | solution.py:373
  60.2 57.1 %shard_map.205 = (bf16[4,256,768]{2,1,0:T(8,128)(2,1)}, f32[4,256,768]{2,1,0:T(8,128)}, bf16[4,256,768]{2,1,0:T(8,128)(2,1)}, bf16[4,256,3072]{2,1,0:T(8,128)(2,...) custom-call(bf16[4,256,768]{2,1,0:T(8,128)(2,1)} %get-tuple-element., ...), custom_call_target="tpu_custom_call" | custom-call | flops 37446746112 | bytes 53168128 | tf_op jit(solution)/shard_map/pallas_call | solution.py:373
  117.3 4.7 %collective-permute-start = (bf16[4,256,896]{2,1,0:T(8,128)(2,1)}, bf16[4,256,896]{2,1,0:T(8,128)(2,1)}, u32[]{:S(2)}, u32[]{:S(2)}) collective-permute-start(bf16[4,256,896]{2,1,0:T(8,128)(2,1)} %get-tuple-element.41.sent_own), channel_id=1, source_target_pairs={{0,1},{1,2},{2,3},{4,5},{5,6},{6,7},{8,9},{9,10},{10,11},{12,13},{... | collective-permute-start | bytes 5505032 | tf_op jit(solution)/shard_map/ppermute | solution.py:504
  122.0 1.3 collective-permute-start.1
  123.3 9.7 %shard_map.212 = bf16[3072,768]{1,0:T(8,128)(2,1)} custom-call(bf16[1024,3072]{1,0:T(8,128)(2,1)} %bitcast.237, bf16[1024,768]{1,0:T(8,128)(2,1)} %bitcast.249), custom_call_target="tpu_custom_call" | custom-call | flops 4831838208 | bytes 12582912 | tf_op jit(solution)/shard_map/pallas_call | solution.py:340
  133.1 4.1 constant_dynamic-slice_fusion.1
  137.2 2.5 copy.78
  139.6 9.2 %shard_map.211 = bf16[768,3072]{1,0:T(8,128)(2,1)} custom-call(bf16[1024,768]{1,0:T(8,128)(2,1)} %bitcast.248, bf16[1024,3072]{1,0:T(8,128)(2,1)} %bitcast.236), custom_call_target="tpu_custom_call" | custom-call | flops 4831838208 | bytes 12582912 | tf_op jit(solution)/shard_map/pallas_call | solution.py:340
  148.9 2.7 constant_dynamic-slice_fusion.3
  151.6 1.6 copy.96
  153.7 4.3 copy.86
  158.1 4.4 %shard_map.210 = bf16[768,768]{1,0:T(8,128)(2,1)} custom-call(bf16[1024,768]{1,0:T(8,128)(2,1)} %bitcast.245, bf16[1024,768]{1,0:T(8,128)(2,1)} %bitcast.246), custom_call_target="tpu_custom_call" | custom-call | flops 1207959552 | bytes 4325376 | tf_op jit(solution)/shard_map/pallas_call | solution.py:340
  162.5 2.6 collective-permute-done.1.sent_next
  165.2 46.4 %shard_map.206 = (f32[4,256,768]{2,1,0:T(8,128)}, bf16[4,256,2304]{2,1,0:T(8,128)(2,1)}, bf16[4,256,2304]{2,1,0:T(8,128)(2,1)}, bf16[4,256,768]{2,1,0:T(8,128)(2,1)}, f32[4,8,768]{2,1,0:T(8,128)}) custom-call(bf16[4,256,768]{2,1,0:T(8,128)(2,1)} %get-tuple-element.37.hb_prev, bf16[4,256,768]{2,1,0:T(8,128)(2,1)} %get-tuple-element.38.hb_next, ...), custom_call_target="tpu_custom_call" | custom-call | flops 19327352832 | bytes 49491968 | tf_op jit(solution)/shard_map/pallas_call | solution.py:373
  212.6 7.7 %shard_map.209 = bf16[768,2304]{1,0:T(8,128)(2,1)} custom-call(bf16[1024,768]{1,0:T(8,128)(2,1)} %bitcast.244, bf16[1024,2304]{1,0:T(8,128)(2,1)} %bitcast.239), custom_call_target="tpu_custom_call" | custom-call | flops 3623878656 | bytes 9830400 | tf_op jit(solution)/shard_map/pallas_call | solution.py:340
  220.3 2.9 pad_maximum_fusion.1
  223.8 1.3 dynamic-slice_bitcast_fusion.3
  225.1 1.6 dynamic-slice_bitcast_fusion.2
  226.8 7.9 %shard_map.207 = bf16[768,2304]{1,0:T(8,128)(2,1)} custom-call(bf16[1024,768]{1,0:T(8,128)(2,1)} %bitcast.243, bf16[1024,2304]{1,0:T(8,128)(2,1)} %bitcast.238), custom_call_target="tpu_custom_call" | custom-call | flops 3623878656 | bytes 9830400 | tf_op jit(solution)/shard_map/pallas_call | solution.py:340
  234.6 4.3 %shard_map.208 = bf16[768,768]{1,0:T(8,128)(2,1)} custom-call(bf16[1024,768]{1,0:T(8,128)(2,1)} %bitcast.242, bf16[1024,768]{1,0:T(8,128)(2,1)} %bitcast.247), custom_call_target="tpu_custom_call" | custom-call | flops 1207959552 | bytes 4325376 | tf_op jit(solution)/shard_map/pallas_call | solution.py:340
  239.0 2.9 pad_maximum_fusion
  241.9 1.9 fusion.77
  243.8 1.5 copy-done.7
  245.3 1.2 dynamic-slice_bitcast_fusion.5
  247.2 6.9 %fusion.36 = f32[12,768]{1,0:T(8,128)S(1)} fusion(bf16[768,6912]{1,0:T(8,128)(2,1)} %param.19, bf16[4,6912]{1,0:T(4,128)(2,1)S(1)} %get-tuple-element.138, bf16[4,6912]{1,0:T(4,128)(2,1)S(1)} %get-tuple-element.137, bf16[4,6912]{1,0:T(4,128)(2,1)S(1)} %convert_element_type.378), kind=kOutput, calls=%fused_computation.96 | convolution fusion | flops 127899648 | bytes 10819584 | tf_op jit(solution)/shard_map/dot_general | solution.py:28
  254.1 17.0 %psum.7 = f32[4,768]{1,0:T(4,128)S(1)} all-reduce(f32[4,768]{1,0:T(4,128)S(1)} %fusion.58), channel_id=1, replica_groups=mesh['clip'=8,'frame'=4] {'frame'}, use_global_device_ids=true, to_apply=%region_0.1 | all-reduce | flops 3072 | bytes 24576 | tf_op jit(solution)/shard_map/psum | solution.py:569
  271.2 9.2 %all-gather = f32[8,4,768]{2,1,0:T(4,128)S(1)} all-gather(f32[1,4,768]{2,1,0:T(4,128)S(1)} %bitcast.232), channel_id=1, replica_groups=mesh['clip'=8,'frame'=4] {'clip'}, dimensions={0}, use_global_device_ids=true | all-gather | bytes 110592 | tf_op jit(solution)/shard_map/all_gather | solution.py:570
  280.4 2.4 dynamic-slice_bitcast_fusion.4
  283.0 2.3 fusion.24
  285.2 2.5 collective-permute-done.3
  287.8 9.3 %all-gather.1 = f32[8,4,1728]{2,1,0:T(4,128)S(1)} all-gather(f32[1,4,1728]{2,1,0:T(4,128)S(1)} %fusion.51), channel_id=1, replica_groups=mesh['clip'=8,'frame'=4] {'clip'}, dimensions={0}, use_global_device_ids=true | all-gather | bytes 248832 | tf_op jit(solution)/shard_map/all_gather | solution.py:577
  297.1 1.1 fusion.30
  298.6 2.9 fusion
  302.3 2.3 fusion.1
  304.8 1.5 collective-permute-start.21
  306.4 1.6 fusion.5
  308.0 1.5 collective-permute-start.13
  309.5 1.5 fusion.4
  311.8 1.6 fusion.7
  313.5 1.4 collective-permute-start.5
  315.3 15.3 %collective-permute-done.26 = bf16[2,384,768]{1,2,0:T(8,128)(2,1)S(1)} collective-permute-done((bf16[2,384,768]{1,2,0:T(8,128)(2,1)S(1)}, bf16[2,384,768]{1,2,0:T(8,128)(2,1)S(1)}, u32[]{:S(2)}, u32[]{:S(2)}) %collective-permute-start.26) | collective-permute-done | bytes 1179680 | tf_op jit(solution)/shard_map/ppermute | solution.py:400
  332.4 1.4 collective-permute-done.21
  333.7 1.5 collective-permute-start.27
  336.5 9.9 %collective-permute-done.13 = bf16[2,96,1536]{2,1,0:T(8,128)(2,1)S(1)} collective-permute-done((bf16[2,96,1536]{2,1,0:T(8,128)(2,1)S(1)}, bf16[2,96,1536]{2,1,0:T(8,128)(2,1)S(1)}, u32[]{:S(2)}, u32[]{:S(2)}) %collective-permute-start.13) | collective-permute-done | bytes 589856 | tf_op jit(solution)/shard_map/ppermute | solution.py:400
  346.4 1.5 collective-permute-start.22
  348.9 10.2 %collective-permute-done.5 = bf16[2,96,1536]{2,1,0:T(8,128)(2,1)S(1)} collective-permute-done((bf16[2,96,1536]{2,1,0:T(8,128)(2,1)S(1)}, bf16[2,96,1536]{2,1,0:T(8,128)(2,1)S(1)}, u32[]{:S(2)}, u32[]{:S(2)}) %collective-permute-start.5) | collective-permute-done | bytes 589856 | tf_op jit(solution)/shard_map/ppermute | solution.py:400
  359.0 1.5 collective-permute-start.17
  363.0 11.9 %collective-permute-done.14 = bf16[96,1536]{1,0:T(8,128)(2,1)S(1)} collective-permute-done((bf16[96,1536]{1,0:T(8,128)(2,1)S(1)}, bf16[96,1536]{1,0:T(8,128)(2,1)S(1)}, u32[]{:S(2)}, u32[]{:S(2)}) %collective-permute-start.14) | collective-permute-done | bytes 294944 | tf_op jit(solution)/shard_map/ppermute | solution.py:400
  375.5 2.0 collective-permute-done.17
  377.6 1.4 reshape.299
  379.2 1.5 maximum_bitcast_fusion.1
  386.1 1.4 reshape.289
  388.6 1.4 maximum_bitcast_fusion
  392.0 1.2 fusion.8
  395.0 1.2 fusion.9
  396.8 1.1 collective-permute-start.23
  399.6 6.3 %collective-permute-done.10 = bf16[2,96,768]{2,1,0:T(8,128)(2,1)} collective-permute-done((bf16[2,96,768]{2,1,0:T(8,128)(2,1)}, bf16[2,96,768]{2,1,0:T(8,128)(2,1)}, u32[]{:S(2)}, u32[]{:S(2)}) %collective-permute-start.10) | collective-permute-done | bytes 294944 | tf_op jit(solution)/shard_map/ppermute | solution.py:400
  407.1 7.2 %collective-permute-done.19 = bf16[96,768]{1,0:T(8,128)(2,1)S(1)} collective-permute-done((bf16[96,768]{1,0:T(8,128)(2,1)S(1)}, bf16[96,768]{1,0:T(8,128)(2,1)S(1)}, u32[]{:S(2)}, u32[]{:S(2)}) %collective-permute-start.19) | collective-permute-done | bytes 147488 | tf_op jit(solution)/shard_map/ppermute | solution.py:400
  415.7 2.0 collective-permute-done.11
  419.4 1.6 collective-permute-start.29
  421.0 1.5 collective-permute-start.24
  422.5 7.3 %collective-permute-done.29 = bf16[384,192]{0,1:T(8,128)(2,1)S(1)} collective-permute-done((bf16[384,192]{0,1:T(8,128)(2,1)S(1)}, bf16[384,192]{0,1:T(8,128)(2,1)S(1)}, u32[]{:S(2)}, u32[]{:S(2)}) %collective-permute-start.29) | collective-permute-done | bytes 147488 | tf_op jit(solution)/shard_map/ppermute | solution.py:400
  430.6 1.1 collective-permute-done.24
  (173 shorter events, 39.5 us)
Async XLA Ops:
  0.6 1.9 copy-start
  3.2 6.3 %copy-start.22 = (s32[4]{0:T(128)S(1)}, s32[4]{0:T(128)}, u32[]{:S(2)}) copy-start(s32[4]{0:T(128)} %param.17) | copy-start | bytes 52
  12.9 46.7 %copy-start.21 = (f32[4]{0:T(128)S(1)}, f32[4]{0:T(128)}, u32[]{:S(2)}) copy-start(f32[4]{0:T(128)} %param.15) | copy-start | bytes 52
  117.3 45.2 %collective-permute-start = (bf16[4,256,896]{2,1,0:T(8,128)(2,1)}, bf16[4,256,896]{2,1,0:T(8,128)(2,1)}, u32[]{:S(2)}, u32[]{:S(2)}) collective-permute-start(bf16[4,256,896]{2,1,0:T(8,128)(2,1)} %get-tuple-element.41.sent_own), channel_id=1, source_target_pairs={{0,1},{1,2},{2,3},{4,5},{5,6},{6,7},{8,9},{9,10},{10,11},{12,13},{... | collective-permute-start | bytes 5505032 | tf_op jit(solution)/shard_map/ppermute | solution.py:504
  122.0 43.1 %collective-permute-start.1 = (bf16[4,256,896]{2,1,0:T(8,128)(2,1)}, bf16[4,256,896]{2,1,0:T(8,128)(2,1)}, u32[]{:S(2)}, u32[]{:S(2)}) collective-permute-start(bf16[4,256,896]{2,1,0:T(8,128)(2,1)} %get-tuple-element.41.sent_own), channel_id=1, source_target_pairs={{1,0},{2,1},{3,2},{5,4},{6,5},{7,6},{9,8},{10,9},{11,10},{13,12},{... | collective-permute-start | bytes 5505032 | tf_op jit(solution)/shard_map/ppermute | solution.py:505
  139.6 158.7 %collective-permute-start.25 = (bf16[2,2,384,768]{2,3,1,0:T(8,128)(2,1)}, bf16[2,2,384,768]{2,3,1,0:T(8,128)(2,1)}, u32[]{:S(2)}, u32[]{:S(2)}) collective-permute-start(bf16[2,2,384,768]{2,3,1,0:T(8,128)(2,1)} %bitcast.217), channel_id=1, source_target_pairs={{0,4},{4,0},{8,12},{12,8},{16,20},{20,16},{24,28},{28,24},{1,5},{5... | collective-permute-start | bytes 7077896 | tf_op jit(solution)/shard_map/ppermute | solution.py:400
  151.6 2.1 copy-start.19
  153.2 148.6 %collective-permute-start.20 = (bf16[2,2,96,3072]{3,2,0,1:T(8,128)(2,1)}, bf16[2,2,96,3072]{3,2,0,1:T(8,128)(2,1)}, u32[]{:S(2)}, u32[]{:S(2)}) collective-permute-start(bf16[2,2,96,3072]{3,2,0,1:T(8,128)(2,1)} %bitcast.202), channel_id=1, source_target_pairs={{0,4},{4,0},{8,12},{12,8},{16,20},{20,16},{24,28},{28,24},{1,5},{5... | collective-permute-start | bytes 7077896 | tf_op jit(solution)/shard_map/ppermute | solution.py:400
  158.0 4.4 %copy-start.20 = (s32[32]{0:T(128)S(1)}, s32[32]{0:T(128)}, u32[]{:S(2)}) copy-start(s32[32]{0:T(128)} %param.16) | copy-start | bytes 388
  223.8 2.9 copy-start.2
  223.8 2.9 copy-start.5
  225.1 79.7 %collective-permute-start.12 = (bf16[2,2,96,1536]{3,2,1,0:T(8,128)(2,1)}, bf16[2,2,96,1536]{3,2,1,0:T(8,128)(2,1)}, u32[]{:S(2)}, u32[]{:S(2)}) collective-permute-start(bf16[2,2,96,1536]{3,2,1,0:T(8,128)(2,1)} %dynamic-slice_bitcast_fusion.3), channel_id=1, source_target_pairs={{0,4},{4,0},{8,12},{12,8},{16,20},{20,16},{24,28},{28,24},{1,5},{5... | collective-permute-start | bytes 3538952 | tf_op jit(solution)/shard_map/ppermute | solution.py:400
  226.7 81.3 %collective-permute-start.15 = (bf16[2,2,96,1536]{3,2,1,0:T(8,128)(2,1)}, bf16[2,2,96,1536]{3,2,1,0:T(8,128)(2,1)}, u32[]{:S(2)}, u32[]{:S(2)}) collective-permute-start(bf16[2,2,96,1536]{3,2,1,0:T(8,128)(2,1)} %dynamic-slice_bitcast_fusion.2), channel_id=1, source_target_pairs={{0,4},{4,0},{8,12},{12,8},{16,20},{20,16},{24,28},{28,24},{1,5},{5... | collective-permute-start | bytes 3538952 | tf_op jit(solution)/shard_map/ppermute | solution.py:400
  243.8 1.5 copy-start.7
  246.8 36.0 %collective-permute-start.2 = (f32[2,4,1728]{2,1,0:T(4,128)S(1)}, f32[2,4,1728]{2,1,0:T(4,128)S(1)}, u32[]{:S(2)}, u32[]{:S(2)}) collective-permute-start(f32[2,4,1728]{2,1,0:T(4,128)S(1)} %bitcast.231), channel_id=1, source_target_pairs={{0,1},{1,0},{2,3},{3,2},{4,5},{5,4},{6,7},{7,6},{8,9},{9,8},{10,11... | collective-permute-start | bytes 165896 | tf_op jit(solution)/shard_map/ppermute | solution.py:400
  282.9 4.8 %collective-permute-start.3 = (f32[4,1728]{1,0:T(4,128)S(1)}, f32[4,1728]{1,0:T(4,128)S(1)}, u32[]{:S(2)}, u32[]{:S(2)}) collective-permute-start(f32[4,1728]{1,0:T(4,128)S(1)} %dynamic-slice_bitcast_fusion.24), channel_id=1, source_target_pairs={{0,2},{1,3},{2,0},{3,1},{4,6},{5,7},{6,4},{7,5},{8,10},{9,11},{10,... | collective-permute-start | bytes 82952 | tf_op jit(solution)/shard_map/ppermute | solution.py:400
  287.7 23.4 %collective-permute-start.4 = (bf16[2,2,96,1536]{3,2,1,0:T(8,128)(2,1)}, bf16[2,2,96,1536]{3,2,1,0:T(8,128)(2,1)}, u32[]{:S(2)}, u32[]{:S(2)}) collective-permute-start(bf16[2,2,96,1536]{3,2,1,0:T(8,128)(2,1)} %dynamic-slice_bitcast_fusion.5), channel_id=1, source_target_pairs={{0,4},{4,0},{8,12},{12,8},{16,20},{20,16},{24,28},{28,24},{1,5},{5... | collective-permute-start | bytes 3538952 | tf_op jit(solution)/shard_map/ppermute | solution.py:400
  298.3 15.2 %collective-permute-start.7 = (bf16[2,2,96,1536]{3,2,1,0:T(8,128)(2,1)}, bf16[2,2,96,1536]{3,2,1,0:T(8,128)(2,1)S(1)}, u32[]{:S(2)}, u32[]{:S(2)}) collective-permute-start(bf16[2,2,96,1536]{3,2,1,0:T(8,128)(2,1)} %dynamic-slice_bitcast_fusion.4), channel_id=1, source_target_pairs={{0,4},{4,0},{8,12},{12,8},{16,20},{20,16},{24,28},{28,24},{1,5},{5... | collective-permute-start | bytes 3538952 | tf_op jit(solution)/shard_map/ppermute | solution.py:400
  301.7 28.9 %collective-permute-start.26 = (bf16[2,384,768]{1,2,0:T(8,128)(2,1)S(1)}, bf16[2,384,768]{1,2,0:T(8,128)(2,1)S(1)}, u32[]{:S(2)}, u32[]{:S(2)}) collective-permute-start(bf16[2,384,768]{1,2,0:T(8,128)(2,1)S(1)} %dynamic-slice_bitcast_fusion), channel_id=1, source_target_pairs={{0,16},{4,20},{8,24},{12,28},{16,0},{20,4},{24,8},{28,12},{1,17},{... | collective-permute-start | bytes 3538952 | tf_op jit(solution)/shard_map/ppermute | solution.py:400
  304.7 1.7 copy-start.6
  304.8 4.7 %copy-start.3 = (bf16[8,96,1536]{2,1,0:T(8,128)(2,1)S(1)}, bf16[8,96,1536]{2,1,0:T(8,128)(2,1)}, u32[]{:S(2)}) copy-start(bf16[8,96,1536]{2,1,0:T(8,128)(2,1)} %copy-done.2) | copy-start | bytes 7077892
  304.8 28.9 %collective-permute-start.21 = (bf16[2,96,3072]{2,1,0:T(8,128)(2,1)S(1)}, bf16[2,96,3072]{2,1,0:T(8,128)(2,1)S(1)}, u32[]{:S(2)}, u32[]{:S(2)}) collective-permute-start(bf16[2,96,3072]{2,1,0:T(8,128)(2,1)S(1)} %dynamic-slice_bitcast_fusion.1), channel_id=1, source_target_pairs={{0,8},{4,12},{8,0},{12,4},{16,24},{20,28},{24,16},{28,20},{1,9},{5... | collective-permute-start | bytes 3538952 | tf_op jit(solution)/shard_map/ppermute | solution.py:400
  308.0 3.9 copy-start.8
  308.0 38.4 %collective-permute-start.13 = (bf16[2,96,1536]{2,1,0:T(8,128)(2,1)S(1)}, bf16[2,96,1536]{2,1,0:T(8,128)(2,1)S(1)}, u32[]{:S(2)}, u32[]{:S(2)}) collective-permute-start(bf16[2,96,1536]{2,1,0:T(8,128)(2,1)S(1)} %dynamic-slice_bitcast_fusion.9), channel_id=1, source_target_pairs={{0,8},{4,12},{8,0},{12,4},{16,24},{20,28},{24,16},{28,20},{1,9},{5... | collective-permute-start | bytes 1769480 | tf_op jit(solution)/shard_map/ppermute | solution.py:400
  311.1 3.8 copy-start.4
  311.2 36.9 %collective-permute-start.16 = (bf16[2,96,1536]{2,1,0:T(8,128)(2,1)S(1)}, bf16[2,96,1536]{2,1,0:T(8,128)(2,1)S(1)}, u32[]{:S(2)}, u32[]{:S(2)}) collective-permute-start(bf16[2,96,1536]{2,1,0:T(8,128)(2,1)S(1)} %dynamic-slice_bitcast_fusion.8), channel_id=1, source_target_pairs={{0,16},{4,20},{8,24},{12,28},{16,0},{20,4},{24,8},{28,12},{1,17},{... | collective-permute-start | bytes 1769480 | tf_op jit(solution)/shard_map/ppermute | solution.py:400
  313.5 45.5 %collective-permute-start.5 = (bf16[2,96,1536]{2,1,0:T(8,128)(2,1)S(1)}, bf16[2,96,1536]{2,1,0:T(8,128)(2,1)S(1)}, u32[]{:S(2)}, u32[]{:S(2)}) collective-permute-start(bf16[2,96,1536]{2,1,0:T(8,128)(2,1)S(1)} %dynamic-slice_bitcast_fusion.11), channel_id=1, source_target_pairs={{0,8},{4,12},{8,0},{12,4},{16,24},{20,28},{24,16},{28,20},{1,9},{5... | collective-permute-start | bytes 1769480 | tf_op jit(solution)/shard_map/ppermute | solution.py:400
  330.6 30.8 %collective-permute-start.8 = (bf16[2,96,1536]{2,1,0:T(8,128)(2,1)S(1)}, bf16[2,96,1536]{2,1,0:T(8,128)(2,1)S(1)}, u32[]{:S(2)}, u32[]{:S(2)}) collective-permute-start(bf16[2,96,1536]{2,1,0:T(8,128)(2,1)S(1)} %dynamic-slice_bitcast_fusion.10), channel_id=1, source_target_pairs={{0,16},{4,20},{8,24},{12,28},{16,0},{20,4},{24,8},{28,12},{1,17},{... | collective-permute-start | bytes 1769480 | tf_op jit(solution)/shard_map/ppermute | solution.py:400
  333.7 58.3 %collective-permute-start.27 = (bf16[384,768]{0,1:T(8,128)(2,1)}, bf16[384,768]{0,1:T(8,128)(2,1)}, u32[]{:S(2)}, u32[]{:S(2)}) collective-permute-start(bf16[384,768]{0,1:T(8,128)(2,1)} %dynamic-slice_bitcast_fusion.6), channel_id=1, source_target_pairs={{0,8},{4,12},{8,0},{12,4},{16,24},{20,28},{24,16},{28,20},{1,9},{5... | collective-permute-start | bytes 1769480 | tf_op jit(solution)/shard_map/ppermute | solution.py:400
  346.4 48.7 %collective-permute-start.22 = (bf16[96,3072]{1,0:T(8,128)(2,1)}, bf16[96,3072]{1,0:T(8,128)(2,1)}, u32[]{:S(2)}, u32[]{:S(2)}) collective-permute-start(bf16[96,3072]{1,0:T(8,128)(2,1)} %dynamic-slice_bitcast_fusion.7), channel_id=1, source_target_pairs={{0,16},{4,20},{8,24},{12,28},{16,0},{20,4},{24,8},{28,12},{1,17},{... | collective-permute-start | bytes 1769480 | tf_op jit(solution)/shard_map/ppermute | solution.py:400
  348.0 26.8 %collective-permute-start.14 = (bf16[96,1536]{1,0:T(8,128)(2,1)S(1)}, bf16[96,1536]{1,0:T(8,128)(2,1)S(1)}, u32[]{:S(2)}, u32[]{:S(2)}) collective-permute-start(bf16[96,1536]{1,0:T(8,128)(2,1)S(1)} %dynamic-slice_bitcast_fusion.16), channel_id=1, source_target_pairs={{0,16},{4,20},{8,24},{12,28},{16,0},{20,4},{24,8},{28,12},{1,17},{... | collective-permute-start | bytes 884744 | tf_op jit(solution)/shard_map/ppermute | solution.py:400
  359.0 18.5 %collective-permute-start.17 = (bf16[96,1536]{1,0:T(8,128)(2,1)S(1)}, bf16[96,1536]{1,0:T(8,128)(2,1)S(1)}, u32[]{:S(2)}, u32[]{:S(2)}) collective-permute-start(bf16[96,1536]{1,0:T(8,128)(2,1)S(1)} %dynamic-slice_bitcast_fusion.15), channel_id=1, source_target_pairs={{0,8},{4,12},{8,0},{12,4},{16,24},{20,28},{24,16},{28,20},{1,9},{5... | collective-permute-start | bytes 884744 | tf_op jit(solution)/shard_map/ppermute | solution.py:400
  360.6 16.9 %copy-start.15 = (bf16[2,96,1536]{2,1,0:T(8,128)(2,1)}, bf16[2,96,1536]{2,1,0:T(8,128)(2,1)S(1)}, u32[]{:S(2)}) copy-start(bf16[2,96,1536]{2,1,0:T(8,128)(2,1)S(1)} %fusion.13) | copy-start | bytes 1769476
  361.5 23.6 %collective-permute-start.6 = (bf16[96,1536]{1,0:T(8,128)(2,1)}, bf16[96,1536]{1,0:T(8,128)(2,1)}, u32[]{:S(2)}, u32[]{:S(2)}) collective-permute-start(bf16[96,1536]{1,0:T(8,128)(2,1)} %dynamic-slice_bitcast_fusion.19), channel_id=1, source_target_pairs={{0,16},{4,20},{8,24},{12,28},{16,0},{20,4},{24,8},{28,12},{1,17},{... | collective-permute-start | bytes 884744 | tf_op jit(solution)/shard_map/ppermute | solution.py:400
  362.2 15.4 %copy-start.17 = (bf16[2,96,1536]{2,1,0:T(8,128)(2,1)}, bf16[2,96,1536]{2,1,0:T(8,128)(2,1)S(1)}, u32[]{:S(2)}) copy-start(bf16[2,96,1536]{2,1,0:T(8,128)(2,1)S(1)} %fusion.12) | copy-start | bytes 1769476
  374.8 8.4 %collective-permute-start.9 = (bf16[96,1536]{1,0:T(8,128)(2,1)}, bf16[96,1536]{1,0:T(8,128)(2,1)}, u32[]{:S(2)}, u32[]{:S(2)}) collective-permute-start(bf16[96,1536]{1,0:T(8,128)(2,1)} %dynamic-slice_bitcast_fusion.18), channel_id=1, source_target_pairs={{0,8},{4,12},{8,0},{12,4},{16,24},{20,28},{24,16},{28,20},{1,9},{5... | collective-permute-start | bytes 884744 | tf_op jit(solution)/shard_map/ppermute | solution.py:400
  379.2 4.1 copy-start.18
  379.2 5.8 %copy-start.16 = (bf16[2,96,1536]{2,1,0:T(8,128)(2,1)S(1)}, bf16[2,96,1536]{2,1,0:T(8,128)(2,1)}, u32[]{:S(2)}) copy-start(bf16[2,96,1536]{2,1,0:T(8,128)(2,1)} %copy-done.15) | copy-start | bytes 1769476
  380.8 0.8 copy-start.9
  382.3 15.6 %collective-permute-start.18 = (bf16[2,96,768]{2,1,0:T(8,128)(2,1)}, bf16[2,96,768]{2,1,0:T(8,128)(2,1)}, u32[]{:S(2)}, u32[]{:S(2)}) collective-permute-start(bf16[2,96,768]{2,1,0:T(8,128)(2,1)} %dynamic-slice_bitcast_fusion.14), channel_id=1, source_target_pairs={{0,1},{1,0},{2,3},{3,2},{4,5},{5,4},{6,7},{7,6},{8,9},{9,8},{10,11... | collective-permute-start | bytes 884744 | tf_op jit(solution)/shard_map/ppermute | solution.py:400
  390.1 3.1 copy-start.11
  390.9 15.0 %collective-permute-start.10 = (bf16[2,96,768]{2,1,0:T(8,128)(2,1)}, bf16[2,96,768]{2,1,0:T(8,128)(2,1)}, u32[]{:S(2)}, u32[]{:S(2)}) collective-permute-start(bf16[2,96,768]{2,1,0:T(8,128)(2,1)} %dynamic-slice_bitcast_fusion.17), channel_id=1, source_target_pairs={{0,1},{1,0},{2,3},{3,2},{4,5},{5,4},{6,7},{7,6},{8,9},{9,8},{10,11... | collective-permute-start | bytes 884744 | tf_op jit(solution)/shard_map/ppermute | solution.py:400
  393.2 3.5 copy-start.13
  394.1 3.9 copy-start.10
  394.1 25.1 %collective-permute-start.28 = (bf16[2,384,192]{1,2,0:T(8,128)(2,1)}, bf16[2,384,192]{1,2,0:T(8,128)(2,1)S(1)}, u32[]{:S(2)}, u32[]{:S(2)}) collective-permute-start(bf16[2,384,192]{1,2,0:T(8,128)(2,1)} %dynamic-slice_bitcast_fusion.12), channel_id=1, source_target_pairs={{0,1},{1,0},{2,3},{3,2},{4,5},{5,4},{6,7},{7,6},{8,9},{9,8},{10,11... | collective-permute-start | bytes 884744 | tf_op jit(solution)/shard_map/ppermute | solution.py:400
  396.3 9.7 %copy-start.12 = (bf16[4,96,768]{2,1,0:T(8,128)(2,1)S(1)}, bf16[4,96,768]{2,1,0:T(8,128)(2,1)}, u32[]{:S(2)}) copy-start(bf16[4,96,768]{2,1,0:T(8,128)(2,1)} %copy-done.11) | copy-start | bytes 1769476
  396.8 22.4 %copy-start.14 = (bf16[384,768]{0,1:T(8,128)(2,1)S(1)}, bf16[384,768]{0,1:T(8,128)(2,1)}, u32[]{:S(2)}) copy-start(bf16[384,768]{0,1:T(8,128)(2,1)} %copy-done.13) | copy-start | bytes 1769476
  396.8 24.1 %collective-permute-start.23 = (bf16[2,96,768]{2,1,0:T(8,128)(2,1)S(1)}, bf16[2,96,768]{2,1,0:T(8,128)(2,1)S(1)}, u32[]{:S(2)}, u32[]{:S(2)}) collective-permute-start(bf16[2,96,768]{2,1,0:T(8,128)(2,1)S(1)} %dynamic-slice_bitcast_fusion.13), channel_id=1, source_target_pairs={{0,1},{1,0},{2,3},{3,2},{4,5},{5,4},{6,7},{7,6},{8,9},{9,8},{10,11... | collective-permute-start | bytes 884744 | tf_op jit(solution)/shard_map/ppermute | solution.py:400
  399.0 15.2 %collective-permute-start.19 = (bf16[96,768]{1,0:T(8,128)(2,1)S(1)}, bf16[96,768]{1,0:T(8,128)(2,1)S(1)}, u32[]{:S(2)}, u32[]{:S(2)}) collective-permute-start(bf16[96,768]{1,0:T(8,128)(2,1)S(1)} %dynamic-slice_bitcast_fusion.22), channel_id=1, source_target_pairs={{0,2},{1,3},{2,0},{3,1},{4,6},{5,7},{6,4},{7,5},{8,10},{9,11},{10,... | collective-permute-start | bytes 442376 | tf_op jit(solution)/shard_map/ppermute | solution.py:400
  407.0 10.7 %collective-permute-start.11 = (bf16[96,768]{1,0:T(8,128)(2,1)S(1)}, bf16[96,768]{1,0:T(8,128)(2,1)S(1)}, u32[]{:S(2)}, u32[]{:S(2)}) collective-permute-start(bf16[96,768]{1,0:T(8,128)(2,1)S(1)} %dynamic-slice_bitcast_fusion.23), channel_id=1, source_target_pairs={{0,2},{1,3},{2,0},{3,1},{4,6},{5,7},{6,4},{7,5},{8,10},{9,11},{10,... | collective-permute-start | bytes 442376 | tf_op jit(solution)/shard_map/ppermute | solution.py:400
  415.0 17.5 %copy-start.1 = (f32[1000,768]{1,0:T(8,128)S(1)}, f32[1000,768]{1,0:T(8,128)}, u32[]{:S(2)}) copy-start(f32[1000,768]{1,0:T(8,128)} %param.18) | copy-start | bytes 9216004
  419.4 10.5 %collective-permute-start.29 = (bf16[384,192]{0,1:T(8,128)(2,1)S(1)}, bf16[384,192]{0,1:T(8,128)(2,1)S(1)}, u32[]{:S(2)}, u32[]{:S(2)}) collective-permute-start(bf16[384,192]{0,1:T(8,128)(2,1)S(1)} %dynamic-slice_bitcast_fusion.20), channel_id=1, source_target_pairs={{0,2},{1,3},{2,0},{3,1},{4,6},{5,7},{6,4},{7,5},{8,10},{9,11},{10,... | collective-permute-start | bytes 442376 | tf_op jit(solution)/shard_map/ppermute | solution.py:400
  421.0 10.7 %collective-permute-start.24 = (bf16[96,768]{1,0:T(8,128)(2,1)S(1)}, bf16[96,768]{1,0:T(8,128)(2,1)S(1)}, u32[]{:S(2)}, u32[]{:S(2)}) collective-permute-start(bf16[96,768]{1,0:T(8,128)(2,1)S(1)} %dynamic-slice_bitcast_fusion.21), channel_id=1, source_target_pairs={{0,2},{1,3},{2,0},{3,1},{4,6},{5,7},{6,4},{7,5},{8,10},{9,11},{10,... | collective-permute-start | bytes 442376 | tf_op jit(solution)/shard_map/ppermute | solution.py:400
